TPU v7x, 32 devices: a whole 2x2x4 slice. The times are simulated.
32 devices in a mesh: ctx: 8 (over z, x), tp: 4 (over y, core).
Axes of the slice: x: 2, y: 2, z: 4, core: 2. Of those that a mesh axis runs over, the one named last changes fastest.
Arguments:
- out_gate: bfloat16 [1024, 8192], P('ctx', 'tp'), may hold values from -128 to 128
- key_proj: bfloat16 [1024, 8192], P('ctx', 'tp'), may hold values from -6 to 6
- value_proj: bfloat16 [1024, 8192], P('ctx', 'tp'), may hold values from -6 to 6
- residue: float32 [512, 16], P('tp'), may hold values from -1 to 1
- log_decay: float32 [512, 16], P('tp'), may hold values from -13 to -3
- skip: float32 [8192], P('tp'), may hold values from -4 to 4
- gain: float32 [8192], P('tp'), may hold values from 0.1 to 1.9
- cotangent: bfloat16 [1024, 8192], P('ctx', 'tp'), may hold values from -6 to 6
Outputs:
- mixer_out: bfloat16 [1024, 8192], P('ctx', 'tp')
- grad_q: bfloat16 [1024, 8192], P('ctx', 'tp')
- grad_k: bfloat16 [1024, 8192], P('ctx', 'tp')
- grad_v: bfloat16 [1024, 8192], P('ctx', 'tp')
- grad_residue: float32 [512, 16], P('tp')
- grad_log_decay: float32 [512, 16], P('tp')
All inputs are finite; a program needn't handle non-finite values.
Results may differ from a plain program's by a relative error of at most 0.0013.
Values sent between devices are 32-bit elements; how exact they have to be, the bound alone decides.
A program may use at most 128 MiB of HBM per device.

v0:
```python
import jax
import jax.numpy as jnp
from jax import lax
from jax.sharding import PartitionSpec as P

EPSILON = 1e-06
HIGHEST_ACCURACY = lax.Precision.HIGHEST


def prefix(value, axis, combine, identity, reverse):
    count, here = (lax.axis_size(axis), lax.axis_index(axis))
    everything = jax.tree.map(lambda part: lax.all_gather(part, axis), value)
    start = jax.tree.map(
        lambda part, zero: jnp.broadcast_to(jnp.asarray(zero, part.dtype), part.shape),
        value,
        identity,
    )

    def step(k, before):
        at = count - 1 - k if reverse else k
        reached = at > here if reverse else at < here
        new = combine(before, jax.tree.map(lambda part: part[at], everything))
        return jax.tree.map(lambda a, b: jnp.where(reached, a, b), new, before)

    return lax.fori_loop(0, count, step, start)


def toeplitz_block(taps_ext, first_row, row_count, span):
    row_ids = first_row + jnp.arange(row_count, dtype=jnp.int32)

    def toeplitz_one_row(row_id):
        return lax.dynamic_slice_in_dim(taps_ext, span - 1 - row_id, span, 0)

    return jax.vmap(toeplitz_one_row)(row_ids)


def shear_rows(product, first_row, span):
    row_count = product.shape[0]
    extended = jnp.concatenate([jnp.flip(product, 1), jnp.zeros_like(product)], axis=1)
    row_ids = first_row + jnp.arange(row_count, dtype=jnp.int32)

    def shear_one_row(row_data, row_id):
        return lax.dynamic_slice_in_dim(row_data, span - 1 - row_id, span, 0)

    return jnp.sum(jax.vmap(shear_one_row)(extended, row_ids), axis=0)


def join_forward(earlier, later_part):
    state_early, moment_early, decay_early, length_early = earlier
    state_late, moment_late, decay_late, length_late = later_part
    factor = decay_late[:, None, :]
    state_new = factor * state_early + state_late
    moment_new = factor * (moment_early + length_late[0] * state_early) + moment_late
    return (state_new, moment_new, decay_early * decay_late, length_early + length_late)


def join_backward(earlier, later_part):
    state_early, decay_early = earlier
    state_late, decay_late = later_part
    return (decay_late[:, None, :] * state_early + state_late, decay_early * decay_late)


def per_device(out_gate, key_proj, value_proj, residue, log_decay, skip, gain, cotangent):
    block_len, channel_count = out_gate.shape
    groups, modes = residue.shape
    members = channel_count // groups
    shard_total = lax.axis_size("ctx")
    token_total = block_len * shard_total
    full_width = channel_count * lax.axis_size("tp")
    sub_len = min(block_len, 128)
    sub_count = block_len // sub_len
    row_block = min(sub_len, 32)
    gate_full = out_gate.astype(jnp.float32)
    key_full = key_proj.astype(jnp.float32)
    value_full = value_proj.astype(jnp.float32)
    signal = key_full * value_full
    grid_signal = signal.reshape(block_len, groups, members).transpose(0, 2, 1)
    rate_table = jnp.exp(log_decay).T
    residue_table = residue.T
    lag_index = jnp.arange(block_len, dtype=jnp.float32)
    head_decay = jnp.exp(-rate_table[:, None, :] * lag_index[None, :, None])
    back_head = jnp.flip(head_decay, 1)
    own_state = jnp.einsum("rsg,scg->rcg", back_head, grid_signal, precision=HIGHEST_ACCURACY)
    own_moment = jnp.einsum(
        "rsg,scg->rcg",
        back_head * jnp.flip(lag_index)[None, :, None],
        grid_signal,
        precision=HIGHEST_ACCURACY,
    )
    step_decay = jnp.exp(-rate_table * block_len)
    zero_state = jnp.zeros_like(own_state)
    own_length = jnp.full((1,), block_len, jnp.float32)
    identity = (zero_state, zero_state, jnp.ones_like(step_decay), jnp.zeros((1,), jnp.float32))
    state_in, moment_in, _, _ = prefix(
        (own_state, own_moment, step_decay, own_length), "ctx", join_forward, identity, False
    )
    sub_signal = grid_signal.reshape(sub_count, sub_len, members, groups)
    sub_index = jnp.arange(sub_len, dtype=jnp.float32)
    segment_head = jnp.exp(-rate_table[:, None, :] * sub_index[None, :, None])
    segment_trail = jnp.exp(-rate_table[:, None, :] * (sub_index + 1.0)[None, :, None])
    sub_back = jnp.flip(segment_head, 1)
    segment_taps = jnp.sum(residue_table[:, None, :] * segment_head, axis=0)
    taps_ext = jnp.concatenate([jnp.flip(segment_taps, 0), jnp.zeros_like(segment_taps)], axis=0)
    block_number = jnp.arange(sub_count, dtype=jnp.float32)
    later_number = block_number[:, None]
    earlier_number = block_number[None, :]
    gap_before = jnp.maximum(later_number - 1.0 - earlier_number, 0.0) * sub_len
    mask_before = (earlier_number < later_number).astype(jnp.float32)
    pass_before = (
        jnp.exp(-rate_table[:, None, None, :] * gap_before[None, :, :, None])
        * mask_before[None, :, :, None]
    )
    start_offset = sub_len * block_number
    start_decay = jnp.exp(-rate_table[:, None, :] * start_offset[None, :, None])
    sub_state = jnp.einsum("rsg,nscg->nrcg", sub_back, sub_signal, precision=HIGHEST_ACCURACY)
    sub_moment = jnp.einsum(
        "rsg,nscg->nrcg",
        sub_back * jnp.flip(sub_index)[None, :, None],
        sub_signal,
        precision=HIGHEST_ACCURACY,
    )
    incoming_state = jnp.einsum(
        "rnig,ircg->nrcg", pass_before, sub_state, precision=HIGHEST_ACCURACY
    )
    incoming_state = incoming_state + jnp.einsum(
        "rng,rcg->nrcg", start_decay, state_in, precision=HIGHEST_ACCURACY
    )
    enter_moment = jnp.einsum(
        "rnig,ircg->nrcg", pass_before, sub_moment, precision=HIGHEST_ACCURACY
    )
    enter_moment = enter_moment + jnp.einsum(
        "rnig,ircg->nrcg",
        pass_before * gap_before[None, :, :, None],
        sub_state,
        precision=HIGHEST_ACCURACY,
    )
    enter_moment = enter_moment + jnp.einsum(
        "rng,rcg->nrcg", start_decay, moment_in, precision=HIGHEST_ACCURACY
    )
    enter_moment = enter_moment + jnp.einsum(
        "rng,rcg->nrcg",
        start_decay * start_offset[None, :, None],
        state_in,
        precision=HIGHEST_ACCURACY,
    )
    carried = jnp.einsum(
        "rug,nrcg->nucg",
        residue_table[:, None, :] * segment_trail,
        incoming_state,
        precision=HIGHEST_ACCURACY,
    )
    matrices = []
    local_parts = []
    for row_start in range(0, sub_len, row_block):
        matrix = toeplitz_block(taps_ext, row_start, row_block, sub_len)
        matrices.append(matrix)
        local_parts.append(
            jnp.einsum("tsg,nscg->ntcg", matrix, sub_signal, precision=HIGHEST_ACCURACY)
        )
    local_grid = jnp.concatenate(local_parts, axis=1) + carried
    convolved = (
        local_grid.reshape(block_len, members, groups)
        .transpose(0, 2, 1)
        .reshape(block_len, channel_count)
    )
    mixed = convolved + skip * signal
    premix = gate_full * mixed
    squares = lax.psum(jnp.sum(premix * premix, axis=1), "tp")
    inverse = lax.rsqrt(squares / full_width + EPSILON)[:, None]
    normed = premix * inverse
    mixer_out = (normed * gain).astype(jnp.bfloat16)
    pull = cotangent.astype(jnp.float32) * gain
    inner = lax.psum(jnp.sum(pull * normed, axis=1), "tp")
    dpre = (pull - normed * (inner / full_width)[:, None]) * inverse
    grad_q = (dpre * mixed).astype(jnp.bfloat16)
    weight = dpre * gate_full
    grid_weight = weight.reshape(block_len, groups, members).transpose(0, 2, 1)
    local_leading_part = jnp.einsum(
        "rsg,scg->rcg", head_decay, grid_weight, precision=HIGHEST_ACCURACY
    )
    after_state, _ = prefix(
        (local_leading_part, step_decay),
        "ctx",
        join_backward,
        (zero_state, jnp.ones_like(step_decay)),
        True,
    )
    segment_weight = grid_weight.reshape(sub_count, sub_len, members, groups)
    gap_after = jnp.maximum(earlier_number - later_number - 1.0, 0.0) * sub_len
    mask_after = (earlier_number > later_number).astype(jnp.float32)
    pass_after = (
        jnp.exp(-rate_table[:, None, None, :] * gap_after[None, :, :, None])
        * mask_after[None, :, :, None]
    )
    end_decay = jnp.exp(
        -rate_table[:, None, :] * (sub_len * (sub_count - 1.0 - block_number))[None, :, None]
    )
    segment_leading = jnp.einsum(
        "rug,nucg->nrcg", segment_head, segment_weight, precision=HIGHEST_ACCURACY
    )
    after_sub = jnp.einsum(
        "rnig,ircg->nrcg", pass_after, segment_leading, precision=HIGHEST_ACCURACY
    )
    after_sub = after_sub + jnp.einsum(
        "rng,rcg->nrcg", end_decay, after_state, precision=HIGHEST_ACCURACY
    )
    back_cross = jnp.einsum(
        "rsg,nrcg->nscg",
        residue_table[:, None, :] * jnp.flip(segment_trail, 1),
        after_sub,
        precision=HIGHEST_ACCURACY,
    )
    back_local = jnp.zeros_like(segment_weight)
    lagged = jnp.zeros((sub_len, groups), jnp.float32)
    for block_id, row_start in enumerate(range(0, sub_len, row_block)):
        band_weight = segment_weight[:, row_start : row_start + row_block]
        back_local = back_local + jnp.einsum(
            "tsg,ntcg->nscg", matrices[block_id], band_weight, precision=HIGHEST_ACCURACY
        )
        product = jnp.einsum("ntcg,nscg->tsg", band_weight, sub_signal, precision=HIGHEST_ACCURACY)
        lagged = lagged + shear_rows(product, row_start, sub_len)
    back_grid = back_local + back_cross
    grad_signal = (
        back_grid.reshape(block_len, members, groups)
        .transpose(0, 2, 1)
        .reshape(block_len, channel_count)
        + skip * weight
    )
    grad_k = (grad_signal * value_full).astype(jnp.bfloat16)
    grad_v = (grad_signal * key_full).astype(jnp.bfloat16)
    pair_sums = jnp.einsum(
        "ntcg,nrcg->rntg", segment_weight, incoming_state, precision=HIGHEST_ACCURACY
    )
    pair_moment = jnp.einsum(
        "ntcg,nrcg->rntg", segment_weight, enter_moment, precision=HIGHEST_ACCURACY
    )
    tail_wide = segment_trail[:, None, :, :]
    residue_part = jnp.sum(tail_wide * pair_sums, axis=(1, 2)) + jnp.sum(
        segment_head * lagged[None], axis=1
    )
    moment_part = jnp.sum(
        tail_wide * ((sub_index + 1.0)[None, None, :, None] * pair_sums + pair_moment), axis=(1, 2)
    )
    moment_part = moment_part + jnp.sum(
        segment_head * sub_index[None, :, None] * lagged[None], axis=1
    )
    residue_total, moment_total = lax.psum((residue_part.T, moment_part.T), "ctx")
    grad_residue = residue_total / token_total
    grad_log_decay = -residue * jnp.exp(log_decay) * moment_total / token_total
    return (mixer_out, grad_q, grad_k, grad_v, grad_residue, grad_log_decay)


def solution(mesh):
    placed = (
        P("ctx", "tp"),
        P("ctx", "tp"),
        P("ctx", "tp"),
        P("tp", None),
        P("tp", None),
        P("tp"),
        P("tp"),
        P("ctx", "tp"),
    )
    return jax.shard_map(
        per_device,
        mesh=mesh,
        in_specs=placed,
        out_specs=(
            P("ctx", "tp"),
            P("ctx", "tp"),
            P("ctx", "tp"),
            P("ctx", "tp"),
            P("tp", None),
            P("tp", None),
        ),
        check_vma=False,
    )
```

profile of v0, /device:TPU:0, one launch (start us, length us, event | category | flops | bytes accessed | tf_op | source)
XLA Modules:
  0.0 867.0 jit_solution(6984951884670089754)
XLA Ops:
  20.3 91.4 %while.39 = (s32[]{:T(128)}, f32[256,128]{1,0:T(8,128)S(1)}, s32[32,2]{0,1:T(2,128)S(1)}, f32[32,128,128]{1,0,2:T(8,128)S(1)}, s32[]{:T(128)}, /*index=5*/s32[]{:T(128)}) while((s32[]{:T(128)}, f32[256,128]{1,0:T(8,128)S(1)}, s32[32,2]{0,1:T(2,128)S(1)}, f32[32,128,128]{1,0,2:T(8,128)S(1)}, s32[]{:T(128)}, /*index=5*/s32[]{:T(128)}) %tuple.158), condition=%wide.while_cond.3, body=%wide.while_body.3.sunk | while | flops 2 | bytes 393329 | solution.py:32
  113.5 137.7 %while.38 = (s32[]{:T(128)}, f32[256,128]{1,0:T(8,128)S(1)}, s32[32,2]{0,1:T(2,128)S(1)}, f32[32,128,128]{1,0,2:T(8,128)}, s32[]{:T(128)}, /*index=5*/s32[]{:T(128)}) while((s32[]{:T(128)}, f32[256,128]{1,0:T(8,128)S(1)}, s32[32,2]{0,1:T(2,128)S(1)}, f32[32,128,128]{1,0,2:T(8,128)}, s32[]{:T(128)}, /*index=5*/s32[]{:T(128)}) %tuple.179), condition=%wide.while_cond.2, body=%wide.while_body.2.sunk | while | flops 2 | bytes 393329 | solution.py:32
  252.8 138.1 %while.37 = (s32[]{:T(128)}, f32[256,128]{1,0:T(8,128)S(1)}, s32[32,2]{0,1:T(2,128)S(1)}, f32[32,128,128]{1,0,2:T(8,128)}, s32[]{:T(128)}, /*index=5*/s32[]{:T(128)}) while((s32[]{:T(128)}, f32[256,128]{1,0:T(8,128)S(1)}, s32[32,2]{0,1:T(2,128)S(1)}, f32[32,128,128]{1,0,2:T(8,128)}, s32[]{:T(128)}, /*index=5*/s32[]{:T(128)}) %tuple.180), condition=%wide.while_cond.1, body=%wide.while_body.1.sunk | while | flops 2 | bytes 393329 | solution.py:32
  393.9 137.7 %while.36 = (s32[]{:T(128)}, f32[256,128]{1,0:T(8,128)S(1)}, s32[32,2]{0,1:T(2,128)S(1)}, f32[32,128,128]{1,0,2:T(8,128)}, s32[]{:T(128)}, /*index=5*/s32[]{:T(128)}) while((s32[]{:T(128)}, f32[256,128]{1,0:T(8,128)S(1)}, s32[32,2]{0,1:T(2,128)S(1)}, f32[32,128,128]{1,0,2:T(8,128)}, s32[]{:T(128)}, /*index=5*/s32[]{:T(128)}) %tuple.181), condition=%wide.while_cond, body=%wide.while_body.sunk | while | flops 2 | bytes 393329 | solution.py:32
  531.5 23.6 %all-reduce.9 = f32[8]{0:T(128)} all-reduce(f32[8]{0:T(128)S(1)} %dynamic-update-slice.8), channel_id=1, replica_groups=mesh['ctx'=8,'tp'=4] {'ctx'}, use_global_device_ids=true, to_apply=%add.9 | all-reduce | flops 8 | bytes 64
  564.4 32.7 %all-gather = f32[128,128]{1,0:T(8,128)} all-gather(f32[16,128]{1,0:T(8,128)S(1)} %get-tuple-element.556), channel_id=2, replica_groups=mesh['ctx'=8,'tp'=4] {'ctx'}, dimensions={0}, use_global_device_ids=true | all-gather | bytes 73728 | tf_op jit(solution)/shard_map/all_gather | solution.py:12
  597.7 4.3 convolution_bitcast_fusion.7
  602.0 4.4 convolution_bitcast_fusion.8
  606.4 4.4 convolution_bitcast_fusion.9
  610.8 4.4 convolution_bitcast_fusion.10
  615.3 24.2 %while.40 = (s32[]{:T(128)}, f32[16,16,128]{2,1,0:T(8,128)S(1)}, f32[16,16,128]{2,1,0:T(8,128)S(1)}, s32[]{:T(128)}, f32[8,16,128]{2,1,0:T(8,128)}, /*index=5*/f...) while((s32[]{:T(128)}, f32[16,16,128]{2,1,0:T(8,128)S(1)}, ...), condition=%wide.region_2.3_spmd.clone, body=%wide.region_1.2_spmd.clone.sunk | while | flops 327684 | bytes 811161 | solution.py:25
  641.7 5.5 fusion.3
  647.7 5.7 psum.28
  654.9 15.1 %psum.29 = f32[128]{0:T(128)S(1)} all-reduce(f32[128]{0:T(128)S(1)} %multiply_reduce_fusion.3), channel_id=1, replica_groups=mesh['ctx'=8,'tp'=4] {'tp'}, use_global_device_ids=true, to_apply=%region_6.7 | all-reduce | flops 128 | bytes 1024 | tf_op jit(solution)/shard_map/psum | solution.py:173
  673.1 5.1 convolution_bitcast_fusion
  678.2 5.1 convolution_bitcast_fusion.1
  683.3 4.8 convolution_bitcast_fusion.3
  688.2 5.3 convolution_bitcast_fusion.2
  738.6 6.1 gather_fusion.3
  750.6 6.1 gather_fusion.2
  762.7 6.1 gather_fusion
  774.8 6.1 gather_fusion.1
  794.6 33.2 %all-reduce.10 = (f32[128,16]{0,1:T(8,128)S(1)}, f32[128,16]{0,1:T(8,128)S(1)}) all-reduce(f32[128,16]{0,1:T(8,128)S(1)} %add_bitcast_fusion.1, f32[128,16]{0,1:T(8,128)S(1)} %add_bitcast_fusion), channel_id=1, replica_groups=mesh['ctx'=8,'tp'=4] {'ctx'}, use_global_device_ids=true, to_apply=%region_15.16 | all-reduce | flops 4096 | bytes 32768 | tf_op jit(solution)/shard_map/psum | solution.py:247
  839.7 13.8 %while.41 = (s32[]{:T(128)}, f32[16,16,128]{2,1,0:T(8,128)S(1)}, s32[]{:T(128)}, f32[8,16,128]{2,1,0:T(8,128)}, f32[8,16,16,128]{3,2,1,0:T(8,128)}, /*index=5*/s32[]{:T(128)}, s32[]{:T(128)}, s32[]{:T(128)}, s32[]{:T(128)}) while((s32[]{:T(128)}, f32[16,16,128]{2,1,0:T(8,128)S(1)}, s32[]{:T(128)}, f32[8,16,128]{2,1,0:T(8,128)}, ...), condition=%wide.region_8.9_spmd.clone, body=%wide.region_7.8_spmd.clone.sunk | while | flops 131080 | bytes 417967 | solution.py:25
  (862 shorter events, 671.1 us)
Async XLA Ops:
  7.2 608.1 %all-gather.8.cloned.1.call-start = ((), (), s32[]{:S(2)}) async-start(), calls=%async_computation | async-start | bytes 1179648 | tf_op jit(solution)/shard_map/all_gather | solution.py:12
  14.5 600.7 %all-gather.10.cloned.1.call-start = ((), (), s32[]{:S(2)}) async-start(), calls=%async_computation.1 | async-start | bytes 1179648 | tf_op jit(solution)/shard_map/all_gather | solution.py:12
  19.7 820.0 %all-gather.12.cloned.1.call-start = ((), (), s32[]{:S(2)}) async-start(), calls=%async_computation.2 | async-start | bytes 1179648 | tf_op jit(solution)/shard_map/all_gather | solution.py:12
  111.7 486.0 %copy-start = (f32[32,128,128]{1,0,2:T(8,128)}, f32[32,128,128]{1,0,2:T(8,128)S(1)}, u32[]{:S(2)}) copy-start(f32[32,128,128]{1,0,2:T(8,128)S(1)} %get-tuple-element.312) | copy-start | bytes 6291460
  251.2 139.7 %copy-start.36 = (u32[32]{0:T(128)S(1)}, u32[32]{0:T(128)}, u32[]{:S(2)}) copy-start(u32[32]{0:T(128)} %constant.276) | copy-start | bytes 388
  610.8 28.7 %copy-start.23 = (f32[128,16,16]{0,1,2:T(8,128)S(1)}, f32[128,16,16]{0,1,2:T(8,128)}, u32[]{:S(2)}) copy-start(f32[128,16,16]{0,1,2:T(8,128)} %copy.253) | copy-start | bytes 393220
  610.8 28.7 %copy-start.24 = (f32[128,16,16]{0,1,2:T(8,128)S(1)}, f32[128,16,16]{0,1,2:T(8,128)}, u32[]{:S(2)}) copy-start(f32[128,16,16]{0,1,2:T(8,128)} %copy.232) | copy-start | bytes 393220
  610.8 28.7 %copy-start.25 = (f32[16,128]{1,0:T(8,128)S(1)}, f32[16,128]{1,0:T(8,128)}, u32[]{:S(2)}) copy-start(f32[16,128]{1,0:T(8,128)} %get-tuple-element.554) | copy-start | bytes 24580
  610.8 28.7 %copy-start.27 = (f32[16,128]{1,0:T(8,128)S(1)}, f32[16,128]{1,0:T(8,128)}, u32[]{:S(2)}) copy-start(f32[16,128]{1,0:T(8,128)} %get-tuple-element.555) | copy-start | bytes 24580
  615.2 26.4 %copy-start.17 = (f32[1,32,16,128]{1,2,3,0:T(8,128)S(1)}, f32[1,32,16,128]{1,2,3,0:T(8,128)}, u32[]{:S(2)}) copy-start(f32[1,32,16,128]{1,2,3,0:T(8,128)} %convolution_bitcast_fusion.7) | copy-start | bytes 786436
  641.7 5.5 copy-start.9
  641.7 5.5 copy-start.11
  641.7 5.5 copy-start.14
  641.7 5.5 copy-start.32
  647.2 6.1 copy-start.31
  647.6 22.4 %copy-start.8 = (f32[128,2048]{0,1:T(8,128)}, f32[128,2048]{0,1:T(8,128)S(1)}, u32[]{:S(2)}) copy-start(f32[128,2048]{0,1:T(8,128)S(1)} %get-tuple-element.541) | copy-start | bytes 3145732
  688.2 5.3 copy-start.20
  783.6 7.1 copy-start.16
  789.2 38.6 %copy-start.30 = (f32[128,16]{0,1:T(8,128)S(1)}, f32[128,16]{0,1:T(8,128)}, u32[]{:S(2)}) copy-start(f32[128,16]{0,1:T(8,128)} %param.16) | copy-start | bytes 24580
  789.2 38.6 %copy-start.34 = (f32[128,16]{0,1:T(8,128)S(1)}, f32[128,16]{0,1:T(8,128)}, u32[]{:S(2)}) copy-start(f32[128,16]{0,1:T(8,128)} %param.15) | copy-start | bytes 24580
  836.5 17.0 %copy-start.26 = (f32[16,128]{1,0:T(8,128)S(1)}, f32[16,128]{1,0:T(8,128)}, u32[]{:S(2)}) copy-start(f32[16,128]{1,0:T(8,128)} %get-tuple-element.554) | copy-start | bytes 24580
  836.5 17.0 %copy-start.28 = (f32[16,128]{1,0:T(8,128)S(1)}, f32[16,128]{1,0:T(8,128)}, u32[]{:S(2)}) copy-start(f32[16,128]{1,0:T(8,128)} %get-tuple-element.555) | copy-start | bytes 24580
  839.7 15.3 %copy-start.18 = (f32[128,16,128]{2,1,0:T(8,128)S(1)}, f32[128,16,128]{2,1,0:T(8,128)}, u32[]{:S(2)}) copy-start(f32[128,16,128]{2,1,0:T(8,128)} %convolution_add_fusion.1) | copy-start | bytes 3145732
  839.7 15.3 %copy-start.22 = (f32[16,128]{0,1:T(8,128)S(1)}, f32[16,128]{0,1:T(8,128)}, u32[]{:S(2)}) copy-start(f32[16,128]{0,1:T(8,128)} %copy-done.21) | copy-start | bytes 24580
  (17 other events, 49.1 us)
Sparse Core Ops, SparseCore 0:
  14.6 42.8 all-gather.7
  59.6 38.9 all-gather.9
  704.1 36.8 all-gather.11
where the time goes:
time: 882 us; the launch traced here: 867 us
  local copies, waits for them, and re-layouts  629 us (71%)
  blocking collectives  110 us (12%)
  matrix products  68.9 us (8%)
  other arithmetic  40.7 us (5%)
  between operations  14.6 us (2%)
    gather x640, local copies, waits for them, and re-layouts  502 us
    unnamed x96, local copies, waits for them, and re-layouts  33.8 us
    psum x1, blocking collectives, per_device(): lax.psum((residue_part.T, moment_part.T), 'ctx')  33.2 us
    all_gather x1, blocking collectives, prefix(): everything = jax.tree.map(lambda part: lax.all_gather(part, axis), value)  32.7 us
    gather x4, local copies, waits for them, and re-layouts, shear_one_row(): return lax.dynamic_slice_in_dim(row_data, span - 1 - row_id, span, 0)  24.5 us
    unnamed x1, blocking collectives  23.6 us
    select_n x16, other arithmetic, step(): return jax.tree.map(lambda a, b: jnp.where(reached, a, b), new, before)  21.8 us
    dot_general x4, matrix products, per_device(): jnp.einsum('ntcg,nscg->tsg', band_weight, sub_signal, precision=HIGHEST_A...  20.4 us
  transfers between devices with their start and end apart: 3, of which 0 were waited for; matrix products, arithmetic and copies ran while one was open for 74% of the time, Pallas kernels for 0%

commit v1 on v0

v1 whole, which is shorter than its diff:
```python
import functools

import jax
import jax.numpy as jnp
from jax import lax
from jax.experimental import pallas as pl
from jax.experimental.pallas import tpu as pltpu
from jax.sharding import PartitionSpec as P

EPSILON = 1e-06
LANES = 128
SUB = 32
F32 = jnp.float32
BF16 = jnp.bfloat16
MESH = pl.DeviceIdType.MESH


def halves(value):
    high = value.astype(BF16)
    return high, (value - high.astype(F32)).astype(BF16)


def dot(a, b):
    return jnp.dot(a, b, preferred_element_type=F32)


def dot_t(a, b):
    return lax.dot_general(a, b, (((1,), (1,)), ((), ())), preferred_element_type=F32)


def product(left, right, multiply=dot):
    rows = left[0].shape[0]
    both = multiply(jnp.concatenate(left, axis=0), right[0])
    return both[:rows] + both[rows:] + multiply(left[0], right[1])


def exact_dot(value, ones):
    rows = value.shape[0]
    high, rest = value.astype(BF16), None
    rest = value - high.astype(F32)
    mid = rest.astype(BF16)
    low = (rest - mid.astype(F32)).astype(BF16)
    out = dot(jnp.concatenate([high, mid, low], axis=0), ones)
    return out[:rows] + out[rows : 2 * rows] + out[2 * rows :]


def iota(shape, dim):
    return lax.broadcasted_iota(jnp.int32, shape, dim)


def kernel(
    ctx_count,
    tp_count,
    full_width,
    modes,
    members,
    gate_ref,
    key_ref,
    value_ref,
    cot_ref,
    skip_ref,
    gain_ref,
    rate_wide_ref,
    res_wide_ref,
    rate_row_ref,
    res_row_ref,
    rate_chan_ref,
    mixer_ref,
    gq_ref,
    gk_ref,
    gv_ref,
    filt_ref,
    mixed_s,
    weight_s,
    back_s,
    sub_s,
    state_s,
    late_s,
    mask_tok,
    mask_mode,
    acc_s,
    total_s,
    own_s,
    in_s,
    out_s,
    got_s,
    own_b,
    in_b,
    out_b,
    got_b,
    norm_own,
    norm_got,
    part_s,
    part_got,
    send_sem,
    recv_sem,
    tp_send,
    tp_recv,
):
    here = lax.axis_index("ctx")
    side = lax.axis_index("tp")
    length, channels = gate_ref.shape
    subs = length // SUB
    blocks = channels // LANES
    in_block = LANES // members
    wide = in_block * SUB
    piece_rows = blocks * modes // ctx_count

    barrier = pltpu.get_barrier_semaphore()
    for d in range(1, ctx_count):
        pl.semaphore_signal(
            barrier, inc=1, device_id={"ctx": lax.rem(here + d, ctx_count)}, device_id_type=MESH
        )
    for d in range(1, tp_count):
        pl.semaphore_signal(
            barrier, inc=1, device_id={"tp": lax.rem(side + d, tp_count)}, device_id_type=MESH
        )

    mask_tok[...] = (
        iota((wide, LANES), 0) // SUB == iota((wide, LANES), 1) // members
    ).astype(F32).astype(BF16)
    mask_mode[...] = (
        iota((in_block * modes, LANES), 0) // modes == iota((in_block * modes, LANES), 1) // members
    ).astype(F32).astype(BF16)
    acc_s[...] = jnp.zeros_like(acc_s)
    total_s[...] = jnp.zeros_like(total_s)

    def lanes(j, width=LANES):
        return pl.ds(pl.multiple_of(j * width, width), width)

    def stack(value, mask):
        copies = mask.shape[0] // value.shape[0]
        return jnp.concatenate([value] * copies, axis=0) * mask

    def tokens_stack(value):
        mask = mask_tok[...]
        return jnp.concatenate(
            [stack(value[n * SUB : (n + 1) * SUB], mask) for n in range(subs)], axis=1
        )

    def carry_product(table, states):
        mask = mask_mode[...]
        split = [halves(s) for s in states]
        right = [
            jnp.concatenate([stack(s[k], mask) for s in split], axis=1) for k in range(2)
        ]
        return product(halves(table), right)

    def put_state(ref, j, value):
        if piece_rows >= modes:
            per = piece_rows // modes
            ref[j // per, pl.ds(pl.multiple_of((j % per) * modes, modes), modes)] = value
        else:
            per = modes // piece_rows
            for q in range(per):
                ref[j * per + q] = value[q * piece_rows : (q + 1) * piece_rows]

    def take_state(ref, j):
        if piece_rows >= modes:
            per = piece_rows // modes
            return ref[j // per, pl.ds(pl.multiple_of((j % per) * modes, modes), modes)]
        per = modes // piece_rows
        return jnp.concatenate([ref[j * per + q] for q in range(per)], axis=0)

    def chan_rate(j):
        return rate_chan_ref[pl.ds(pl.multiple_of(j * modes, modes), modes)]

    def signal_of(j):
        at = lanes(j)
        return key_ref[:, at].astype(F32) * value_ref[:, at].astype(F32)

    def strided(row, first):
        parts = []
        for h in range(wide // LANES):
            part = jnp.broadcast_to(row[:, h * LANES : (h + 1) * LANES], (SUB, LANES))
            parts.append(pltpu.roll(part, first, 1, stride=1, stride_axis=0))
        return jnp.concatenate(parts, axis=1)

    row_id = iota((SUB, wide), 0)
    lane_id = iota((SUB, wide), 1) % SUB
    offset = (iota((modes, wide), 1) % SUB).astype(F32)

    def first_pass(j, _):
        at = lanes(j)
        rate = rate_wide_ref[:, lanes(j, wide)]
        res = res_wide_ref[:, lanes(j, wide)]
        ending = jnp.exp(-rate * (SUB - offset))
        taps = jnp.sum(res * jnp.exp(-rate * (SUB - 1.0 - offset)), axis=0, keepdims=True)
        toeplitz = jnp.where(lane_id <= row_id, strided(taps, LANES - SUB + 1), 0.0)
        table = jnp.concatenate([toeplitz, ending, ending * (SUB - offset)], axis=0)
        high, low = halves(signal_of(j))
        out = product(halves(table), (tokens_stack(high), tokens_stack(low)))
        for n in range(subs):
            mixed_s[n * SUB : (n + 1) * SUB, at] = out[:SUB, n * LANES : (n + 1) * LANES]
        sub_s[j] = out[SUB:]
        step = jnp.exp(-chan_rate(j) * SUB)
        state = out[SUB : SUB + modes, :LANES]
        for n in range(1, subs):
            state = step * state + out[SUB : SUB + modes, n * LANES : (n + 1) * LANES]
        put_state(own_s, j, state)
        return 0

    lax.fori_loop(0, blocks, first_pass, 0)
    pl.semaphore_wait(barrier, ctx_count - 1 + tp_count - 1)

    def spread(source, target, phase, by_target):
        copies = []
        for d in range(1, ctx_count):
            there = lax.rem(here + d, ctx_count)
            copy = pltpu.make_async_remote_copy(
                src_ref=source.at[there] if by_target else source,
                dst_ref=target.at[here],
                send_sem=send_sem.at[phase, d],
                recv_sem=recv_sem.at[phase, d],
                device_id={"ctx": there},
                device_id_type=MESH,
            )
            copy.start()
            copies.append(copy)
        target[here] = source[here] if by_target else source[...]
        for copy in copies:
            copy.wait()

    def owned_decay():
        if piece_rows >= modes:
            per = piece_rows // modes
            return jnp.exp(
                -length * rate_chan_ref[pl.ds(pl.multiple_of(here * piece_rows, piece_rows), piece_rows)]
            )
        per = modes // piece_rows
        whole = rate_chan_ref[pl.ds(pl.multiple_of(here // per * modes, modes), modes)]
        rates = whole[:piece_rows]
        for q in range(1, per):
            rates = jnp.where(
                here % per == q, whole[q * piece_rows : (q + 1) * piece_rows], rates
            )
        return jnp.exp(-length * rates)

    def join(source, target, reverse):
        decay = owned_decay()

        def step(k, state):
            at = ctx_count - 1 - k if reverse else k
            target[at] = state
            return decay * state + source[at]

        lax.fori_loop(0, ctx_count, step, jnp.zeros((piece_rows, LANES), F32), unroll=True)

    spread(own_s, in_s, 0, True)
    join(in_s, out_s, False)
    spread(out_s, got_s, 1, True)

    time = (iota((SUB, in_block * modes), 0)).astype(F32)

    def second_pass(j, _):
        at = lanes(j)
        step = jnp.exp(-chan_rate(j) * SUB)
        state, moment = take_state(got_s, j), jnp.zeros((modes, LANES), F32)
        states = []
        for n in range(subs):
            states.append(state)
            state_s[j, n] = jnp.concatenate([state, moment], axis=0)
            part = sub_s[j, :, n * LANES : (n + 1) * LANES]
            moment = step * (moment + SUB * state) + part[modes:]
            state = step * state + part[:modes]
        late_s[j] = moment
        rate = rate_row_ref[pl.ds(j, 1)]
        table = res_row_ref[pl.ds(j, 1)] * jnp.exp(-rate * time)
        carried = carry_product(table, states)
        carried = jnp.concatenate(
            [carried[:, n * LANES : (n + 1) * LANES] for n in range(subs)], axis=0
        )
        mixed = mixed_s[:, at] + carried + skip_ref[:, at] * signal_of(j)
        mixed_s[:, at] = mixed
        premix = gate_ref[:, at].astype(F32) * mixed
        pull = cot_ref[:, at].astype(F32) * gain_ref[:, at]
        acc_s[0] += premix * premix
        acc_s[1] += pull * premix
        return 0

    lax.fori_loop(0, blocks, second_pass, 0)

    for k in range(2):
        row = jnp.sum(acc_s[k].T, axis=0, keepdims=True)
        norm_own[4 * k : 4 * k + 4] = jnp.broadcast_to(row, (4, length))
    copies = []
    for d in range(1, tp_count):
        copy = pltpu.make_async_remote_copy(
            src_ref=norm_own,
            dst_ref=norm_got.at[side],
            send_sem=tp_send.at[d],
            recv_sem=tp_recv.at[d],
            device_id={"tp": lax.rem(side + d, tp_count)},
            device_id_type=MESH,
        )
        copy.start()
        copies.append(copy)
    norm_got[side] = norm_own[...]
    for copy in copies:
        copy.wait()
    sums = norm_got[0]
    for k in range(1, tp_count):
        sums = sums + norm_got[k]
    square_row = lax.rsqrt(sums[0:1] / full_width + EPSILON)
    inner_row = sums[4:5] * square_row / full_width
    acc_s[0] = jnp.broadcast_to(square_row, (LANES, length)).T
    acc_s[1] = jnp.broadcast_to(inner_row, (LANES, length)).T

    group_of_lane = iota((LANES, LANES), 0) // members
    group_of_wide = iota((wide, LANES), 0) // SUB
    lane_of = iota((LANES, LANES), 1)
    lane_of_wide = iota((wide, LANES), 1)
    half_row = iota((SUB, LANES), 0)

    def third_pass(j, _):
        at = lanes(j)
        inverse, inner = acc_s[0], acc_s[1]
        mixed = mixed_s[:, at]
        gate = gate_ref[:, at].astype(F32)
        gain = gain_ref[:, at]
        normed = gate * mixed * inverse
        mixer_ref[:, at] = (normed * gain).astype(BF16)
        dpre = (cot_ref[:, at].astype(F32) * gain - normed * inner) * inverse
        gq_ref[:, at] = (dpre * mixed).astype(BF16)
        weight = dpre * gate
        weight_s[:, at] = weight
        rate = rate_wide_ref[:, lanes(j, wide)]
        res = res_wide_ref[:, lanes(j, wide)]
        start = jnp.exp(-rate * offset)
        taps = jnp.sum(res * start, axis=0, keepdims=True)
        toeplitz = jnp.where(lane_id >= row_id, strided(taps, 0), 0.0)
        table = jnp.concatenate([toeplitz, start, start * offset], axis=0)
        high, low = halves(weight)
        right = (tokens_stack(high), tokens_stack(low))
        out = product(halves(table), right)
        for n in range(subs):
            back_s[n * SUB : (n + 1) * SUB, at] = out[:SUB, n * LANES : (n + 1) * LANES]
        sub_s[j] = out[SUB:]
        step = jnp.exp(-chan_rate(j) * SUB)
        last = (subs - 1) * LANES
        state = out[SUB : SUB + modes, last:]
        for n in range(subs - 2, -1, -1):
            state = step * state + out[SUB : SUB + modes, n * LANES : (n + 1) * LANES]
        put_state(own_b, j, state)

        signal = signal_of(j)
        left = tuple(
            jnp.concatenate([part[n * SUB : (n + 1) * SUB] for n in range(subs)], axis=1)
            for part in halves(signal)
        )
        pairs = jnp.where(lane_id >= row_id, product(left, right, dot_t), 0.0)
        lagged = []
        for h in range(wide // LANES):
            part = pairs[:, h * LANES : (h + 1) * LANES]
            bit = 1
            while bit < SUB:
                moved = pltpu.roll(part, LANES - bit, 1)
                part = jnp.where((half_row // bit) % 2 == 1, moved, part)
                bit *= 2
            lagged.append(jnp.sum(part, axis=0, keepdims=True))
        lagged = jnp.concatenate(lagged, axis=1)
        zeroth = start * lagged
        local = jnp.concatenate([zeroth, zeroth * offset], axis=0)
        to_group = (group_of_wide + j * in_block == lane_of_wide).astype(F32).astype(BF16)
        total = exact_dot(local, to_group)

        cross = jnp.zeros((modes, LANES), F32)
        cross_moment = jnp.zeros((modes, LANES), F32)
        for n in range(subs):
            part = out[SUB:, n * LANES : (n + 1) * LANES]
            both = state_s[j, n]
            cross += part[:modes] * both[:modes]
            cross_moment += part[modes:] * both[:modes] + part[:modes] * both[modes:]
        to_group = (group_of_lane + j * in_block == lane_of).astype(F32).astype(BF16)
        total += exact_dot(jnp.concatenate([cross, cross_moment], axis=0), to_group)
        total_s[...] += total
        return 0

    lax.fori_loop(0, blocks, third_pass, 0)

    spread(own_b, in_b, 2, True)
    join(in_b, out_b, True)
    spread(out_b, got_b, 3, True)

    def fourth_pass(j, _):
        at = lanes(j)
        step = jnp.exp(-chan_rate(j) * SUB)
        state = take_state(got_b, j)
        to_group = (group_of_lane + j * in_block == lane_of).astype(F32).astype(BF16)
        total_s[modes:] += exact_dot(state * late_s[j], to_group)
        states = []
        for n in range(subs - 1, -1, -1):
            states.append(state)
            state = step * state + sub_s[j, :modes, n * LANES : (n + 1) * LANES]
        states.reverse()
        rate = rate_row_ref[pl.ds(j, 1)]
        table = res_row_ref[pl.ds(j, 1)] * jnp.exp(-rate * (SUB - time))
        carried = carry_product(table, states)
        carried = jnp.concatenate(
            [carried[:, n * LANES : (n + 1) * LANES] for n in range(subs)], axis=0
        )
        grad = back_s[:, at] + carried + skip_ref[:, at] * weight_s[:, at]
        gk_ref[:, at] = (grad * value_ref[:, at].astype(F32)).astype(BF16)
        gv_ref[:, at] = (grad * key_ref[:, at].astype(F32)).astype(BF16)
        return 0

    lax.fori_loop(0, blocks, fourth_pass, 0)

    part_s[...] = total_s[...]
    spread(part_s, part_got, 4, False)
    sums = part_got[0]
    for k in range(1, ctx_count):
        sums = sums + part_got[k]
    filt_ref[...] = sums


def per_device(out_gate, key_proj, value_proj, residue, log_decay, skip, gain, cotangent):
    length, channels = out_gate.shape
    groups, modes = residue.shape
    members = channels // groups
    ctx_count, tp_count = lax.axis_size("ctx"), lax.axis_size("tp")
    blocks = channels // LANES
    in_block = LANES // members
    subs = length // SUB
    wide = in_block * SUB
    piece_rows = blocks * modes // ctx_count
    rate = jnp.exp(log_decay)
    rate_wide = jnp.repeat(rate.T, SUB, axis=1)
    res_wide = jnp.repeat(residue.T, SUB, axis=1)
    rate_row = rate.reshape(blocks, in_block * modes)
    res_row = residue.reshape(blocks, in_block * modes)
    rate_chan = (
        jnp.repeat(rate.T, members, axis=1)
        .reshape(modes, blocks, LANES)
        .transpose(1, 0, 2)
        .reshape(blocks * modes, LANES)
    )
    pieces = pltpu.VMEM((ctx_count, piece_rows, LANES), F32)
    wide_out = jax.ShapeDtypeStruct((length, channels), BF16)
    vmem = pl.BlockSpec(memory_space=pltpu.VMEM)
    mixer_out, grad_q, grad_k, grad_v, filt = pl.pallas_call(
        functools.partial(
            kernel, ctx_count, tp_count, float(channels * tp_count), modes, members
        ),
        out_shape=[wide_out] * 4 + [jax.ShapeDtypeStruct((2 * modes, groups), F32)],
        in_specs=[vmem] * 11,
        out_specs=[vmem] * 5,
        scratch_shapes=[
            pltpu.VMEM((length, channels), F32),
            pltpu.VMEM((length, channels), F32),
            pltpu.VMEM((length, channels), F32),
            pltpu.VMEM((blocks, 2 * modes, subs * LANES), F32),
            pltpu.VMEM((blocks, subs, 2 * modes, LANES), F32),
            pltpu.VMEM((blocks, modes, LANES), F32),
            pltpu.VMEM((wide, LANES), BF16),
            pltpu.VMEM((in_block * modes, LANES), BF16),
            pltpu.VMEM((2, length, LANES), F32),
            pltpu.VMEM((2 * modes, groups), F32),
            pieces, pieces, pieces, pieces,
            pieces, pieces, pieces, pieces,
            pltpu.VMEM((8, length), F32),
            pltpu.VMEM((tp_count, 8, length), F32),
            pltpu.VMEM((2 * modes, groups), F32),
            pltpu.VMEM((ctx_count, 2 * modes, groups), F32),
            pltpu.SemaphoreType.DMA((5, ctx_count)),
            pltpu.SemaphoreType.DMA((5, ctx_count)),
            pltpu.SemaphoreType.DMA((tp_count,)),
            pltpu.SemaphoreType.DMA((tp_count,)),
        ],
        compiler_params=pltpu.CompilerParams(
            collective_id=0, has_side_effects=True, vmem_limit_bytes=48 * 1024 * 1024
        ),
        name="mixer",
    )(
        out_gate, key_proj, value_proj, cotangent, skip[None], gain[None],
        rate_wide, res_wide, rate_row, res_row, rate_chan,
    )
    token_total = length * ctx_count
    grad_residue = filt[:modes].T / token_total
    grad_log_decay = -residue * rate * filt[modes:].T / token_total
    return mixer_out, grad_q, grad_k, grad_v, grad_residue, grad_log_decay


def solution(mesh):
    wide, table, row = P("ctx", "tp"), P("tp", None), P("tp")
    return jax.shard_map(
        per_device,
        mesh=mesh,
        in_specs=(wide, wide, wide, table, table, row, row, wide),
        out_specs=(wide, wide, wide, wide, table, table),
        check_vma=False,
    )
```

time: 882 us -> 69.2 us (0.08); the launches traced: 867 us -> 68.9 us
  local copies, waits for them, and re-layouts: 629 us -> 10.2 us
  blocking collectives: 110 us -> 0 us
  matrix products: 68.9 us -> 0 us
  Pallas kernels: 0 us -> 56.7 us
  other arithmetic: 40.7 us -> 1.21 us
  between operations: 14.6 us -> 0.76 us
    gather x644 -> x0, local copies, waits for them, and re-layouts: 526 us -> none
    dot_general x19 -> x0, matrix products: 68.9 us -> none  [the longest x4 20.4 us: per_device(): jnp.einsum('ntcg,nscg->tsg', band_weight, sub_signal, precision=HIGHEST_A...]
    pallas_call x0 -> x1, Pallas kernels: none -> 56.7 us  [per_device(): pl.pallas_call(functools.partial(kernel, ctx_count, tp_count, float(chann...]
    psum x3 -> x0, blocking collectives: 54 us -> none  [the longest x1 33.2 us: per_device(): lax.psum((residue_part.T, moment_part.T), 'ctx')]
    all_gather x1 -> x0, blocking collectives: 32.7 us -> none  [prefix(): everything = jax.tree.map(lambda part: lax.all_gather(part, axis), value)]
    unnamed x96 -> x21, local copies, waits for them, and re-layouts: 33.8 us -> 4.6 us
    unnamed x1 -> x0, blocking collectives: 23.6 us -> none
    select_n x20 -> x0, other arithmetic: 21.8 us -> none  [the longest x16 21.8 us: step(): return jax.tree.map(lambda a, b: jnp.where(reached, a, b), new, before)]
  transfers between devices with their start and end apart: 3 -> 0, of which waited for: 0 -> 0; matrix products, arithmetic and copies ran while one was open for 74% -> 0% of each run, Pallas kernels for 0% -> 0%
where the time goes in v1:
time: 69.2 us; the launch traced here: 68.9 us
  Pallas kernels  56.7 us (82%)
  local copies, waits for them, and re-layouts  10.2 us (15%)
  other arithmetic  1.21 us (2%)
  between operations  0.76 us (1%)
    pallas_call x1, Pallas kernels, per_device(): pl.pallas_call(functools.partial(kernel, ctx_count, tp_count, float(chann...  56.7 us
    unnamed x21, local copies, waits for them, and re-layouts  4.6 us
    reshape x1, local copies, waits for them, and re-layouts, per_device(): res_wide = jnp.repeat(residue.T, SUB, axis=1)  1.8 us

profile of v1, /device:TPU:0, one launch (start us, length us, event | category | flops | bytes accessed | tf_op | source)
XLA Modules:
  0.0 68.9 jit_solution(17868136235922656443)
XLA Ops:
  0.6 0.7 %fusion.1 = (f32[128,16]{0,1:T(8,128)S(1)}, f32[16,128]{1,0:T(8,128)S(1)}) fusion(f32[128,16]{0,1:T(8,128)} %param.12), kind=kLoop, calls=%fused_computation.4 | loop fusion | bytes 24576 | tf_op jit(solution)/shard_map/exp | solution.py:427
  1.3 0.1 copy.16
  1.4 0.0 copy-start.6
  1.4 0.1 reshape.29.rate_row_ref
  1.5 0.6 copy-done.6
  2.1 0.1 copy.17
  2.2 0.1 reshape.30.res_row_ref
  2.3 0.3 broadcast_in_dim.19
  2.7 0.3 reshape_reshape.3
  3.0 0.3 broadcast_in_dim.17
  3.4 0.5 reshape.27.rate_wide_ref
  3.9 0.0 copy-start.2
  3.9 0.0 copy-start.3
  3.9 1.3 %broadcast_in_dim.18 = f32[16,128,32]{2,1,0:T(8,128)} broadcast(f32[16,128]{1,0:T(8,128)S(1)} %bitcast.17), dimensions={0,1} | broadcast | bytes 270336 | tf_op jit(solution)/shard_map/broadcast_in_dim | solution.py:429
  5.2 1.8 %reshape.28.res_wide_ref = f32[16,4096]{1,0:T(8,128)S(1)} reshape(f32[16,128,32]{2,1,0:T(8,128)} %broadcast_in_dim.18) | data formatting | bytes 524288 | tf_op jit(solution)/shard_map/reshape | solution.py:429
  7.0 56.7 %mixer.1 = (bf16[128,2048]{1,0:T(8,128)(2,1)S(1)}, bf16[128,2048]{1,0:T(8,128)(2,1)S(1)}, bf16[128,2048]{1,0:T(8,128)(2,1)S(1)}, bf16[128,2048]{1,0:T(8,128)(2,1)S(1)}, f32[32,128]{1,0:T(8,128)S(1)}) custom-call(bf16[128,2048]{1,0:T(8,128)(2,1)S(1)} %copy-done, bf16[128,2048]{1,0:T(8,128)(2,1)S(1)} %copy-done.1, bf16[128,2048]{1,0:T(8,128)(2,1)S(1)} %copy-done.2, ...), custom_call_target="tpu_custom_call" | custom-call | tf_op jit(solution)/shard_map/mixer/pallas_call | solution.py:441
  63.8 0.0 copy-start.7
  63.8 0.7 copy-done.7
  64.5 0.6 fusion
  65.1 0.6 multiply_bitcast_fusion
  65.7 0.8 %copy.23 = bf16[128,2048]{1,0:T(8,128)(2,1)} copy(bf16[128,2048]{1,0:T(8,128)(2,1)S(1)} %get-tuple-element.24) | data formatting | bytes 1048576
  66.5 0.8 %copy.24 = bf16[128,2048]{1,0:T(8,128)(2,1)} copy(bf16[128,2048]{1,0:T(8,128)(2,1)S(1)} %get-tuple-element.25) | data formatting | bytes 1048576
  67.3 0.8 %copy.25 = bf16[128,2048]{1,0:T(8,128)(2,1)} copy(bf16[128,2048]{1,0:T(8,128)(2,1)S(1)} %get-tuple-element.26) | data formatting | bytes 1048576
  68.1 0.8 %copy.26 = bf16[128,2048]{1,0:T(8,128)(2,1)} copy(bf16[128,2048]{1,0:T(8,128)(2,1)S(1)} %get-tuple-element.27) | data formatting | bytes 1048576
  (11 shorter events, 0.1 us)
Async XLA Ops:
  1.4 0.7 %copy-start.6 = (f32[128,16]{0,1:T(8,128)S(1)}, f32[128,16]{0,1:T(8,128)}, u32[]{:S(2)}) copy-start(f32[128,16]{0,1:T(8,128)} %param.11) | copy-start | bytes 24580
  3.9 3.1 %copy-start.2 = (bf16[128,2048]{1,0:T(8,128)(2,1)S(1)}, bf16[128,2048]{1,0:T(8,128)(2,1)}, u32[]{:S(2)}) copy-start(bf16[128,2048]{1,0:T(8,128)(2,1)} %value_ref.1) | copy-start | bytes 1572868
  3.9 3.1 %copy-start.3 = (bf16[128,2048]{1,0:T(8,128)(2,1)S(1)}, bf16[128,2048]{1,0:T(8,128)(2,1)}, u32[]{:S(2)}) copy-start(bf16[128,2048]{1,0:T(8,128)(2,1)} %cot_ref.1) | copy-start | bytes 1572868
  5.2 1.8 %copy-start = (bf16[128,2048]{1,0:T(8,128)(2,1)S(1)}, bf16[128,2048]{1,0:T(8,128)(2,1)}, u32[]{:S(2)}) copy-start(bf16[128,2048]{1,0:T(8,128)(2,1)} %gate_ref.1) | copy-start | bytes 1572868
  5.2 1.8 %copy-start.1 = (bf16[128,2048]{1,0:T(8,128)(2,1)S(1)}, bf16[128,2048]{1,0:T(8,128)(2,1)}, u32[]{:S(2)}) copy-start(bf16[128,2048]{1,0:T(8,128)(2,1)} %key_ref.1) | copy-start | bytes 1572868
  5.2 1.8 %copy-start.4 = (f32[2048]{0:T(1024)S(1)}, f32[2048]{0:T(1024)}, u32[]{:S(2)}) copy-start(f32[2048]{0:T(1024)} %param.13) | copy-start | bytes 24580
  5.2 1.9 %copy-start.5 = (f32[2048]{0:T(1024)S(1)}, f32[2048]{0:T(1024)}, u32[]{:S(2)}) copy-start(f32[2048]{0:T(1024)} %param.14) | copy-start | bytes 24580
  63.8 0.7 %copy-start.7 = (f32[128,16]{0,1:T(8,128)S(1)}, f32[128,16]{0,1:T(8,128)}, u32[]{:S(2)}) copy-start(f32[128,16]{0,1:T(8,128)} %param.12) | copy-start | bytes 24580

commit v2 on v1

v2 whole, which is shorter than its diff:
```python
import functools

import jax
import jax.numpy as jnp
from jax import lax
from jax.experimental import pallas as pl
from jax.experimental.pallas import tpu as pltpu
from jax.sharding import PartitionSpec as P

EPSILON = 1e-06
LANES = 128
SUB = 32
F32 = jnp.float32
BF16 = jnp.bfloat16
MESH = pl.DeviceIdType.MESH


def halves(value):
    high = value.astype(BF16)
    return high, (value - high.astype(F32)).astype(BF16)


def dot(a, b):
    return jnp.dot(a, b, preferred_element_type=F32)


def dot_t(a, b):
    return lax.dot_general(a, b, (((1,), (1,)), ((), ())), preferred_element_type=F32)


def product(left, right, multiply=dot):
    rows = left[0].shape[0]
    both = multiply(jnp.concatenate(left, axis=0), right[0])
    return both[:rows] + both[rows:] + multiply(left[0], right[1])


def exact_dot(value, ones):
    rows = value.shape[0]
    high, rest = value.astype(BF16), None
    rest = value - high.astype(F32)
    mid = rest.astype(BF16)
    low = (rest - mid.astype(F32)).astype(BF16)
    out = dot(jnp.concatenate([high, mid, low], axis=0), ones)
    return out[:rows] + out[rows : 2 * rows] + out[2 * rows :]


def iota(shape, dim):
    return lax.broadcasted_iota(jnp.int32, shape, dim)


def transposed(value, eye):
    high = value.astype(BF16)
    rest = value - high.astype(F32)
    mid = rest.astype(BF16)
    low = (rest - mid.astype(F32)).astype(BF16)
    return dot_t(eye, high) + dot_t(eye, mid) + dot_t(eye, low)


def unit(size):
    return (iota((size, size), 0) == iota((size, size), 1)).astype(F32).astype(BF16)


def kernel(
    ctx_count,
    tp_count,
    full_width,
    gate_ref,
    key_ref,
    value_ref,
    cot_ref,
    skip_ref,
    gain_ref,
    res_ref,
    log_ref,
    mixer_ref,
    gq_ref,
    gk_ref,
    gv_ref,
    filt_ref,
    mixed_s,
    weight_s,
    back_s,
    sub_s,
    state_s,
    late_s,
    mask_tok,
    mask_mode,
    widen,
    wide_s,
    row_s,
    acc_s,
    total_s,
    own_s,
    in_s,
    out_s,
    got_s,
    own_b,
    in_b,
    out_b,
    got_b,
    norm_own,
    norm_got,
    part_s,
    part_got,
    send_sem,
    recv_sem,
    tp_send,
    tp_recv,
):
    here = lax.axis_index("ctx")
    side = lax.axis_index("tp")
    length, channels = gate_ref.shape
    modes, groups = res_ref.shape
    members = channels // groups
    subs = length // SUB
    blocks = channels // LANES
    in_block = LANES // members
    wide = in_block * SUB
    piece_rows = blocks * modes // ctx_count
    per = piece_rows // modes

    barrier = pltpu.get_barrier_semaphore()
    for d in range(1, ctx_count):
        pl.semaphore_signal(
            barrier, inc=1, device_id={"ctx": lax.rem(here + d, ctx_count)}, device_id_type=MESH
        )
    for d in range(1, tp_count):
        pl.semaphore_signal(
            barrier, inc=1, device_id={"tp": lax.rem(side + d, tp_count)}, device_id_type=MESH
        )

    mask_tok[...] = (
        iota((wide, LANES), 0) // SUB == iota((wide, LANES), 1) // members
    ).astype(F32).astype(BF16)
    mask_mode[...] = (
        iota((in_block * modes, LANES), 0) // modes == iota((in_block * modes, LANES), 1) // members
    ).astype(F32).astype(BF16)
    widen[:, :wide] = (iota((groups, wide), 0) == iota((groups, wide), 1) // SUB).astype(F32).astype(BF16)
    widen[:, wide:] = (
        iota((groups, LANES), 0) == iota((groups, LANES), 1) // members
    ).astype(F32).astype(BF16)
    acc_s[...] = jnp.zeros_like(acc_s)
    total_s[...] = jnp.zeros_like(total_s)

    def lanes(j, width=LANES):
        return pl.ds(pl.multiple_of(j * width, width), width)

    def stack(value, mask):
        copies = mask.shape[0] // value.shape[0]
        return jnp.concatenate([value] * copies, axis=0) * mask

    def tokens_stack(value):
        mask = mask_tok[...]
        return jnp.concatenate(
            [stack(value[n * SUB : (n + 1) * SUB], mask) for n in range(subs)], axis=1
        )

    def carry_product(table, states):
        mask = mask_mode[...]
        split = [halves(s) for s in states]
        right = [
            jnp.concatenate([stack(s[k], mask) for s in split], axis=1) for k in range(2)
        ]
        out = product(halves(table), right)
        return jnp.concatenate(
            [out[:, n * LANES : (n + 1) * LANES] for n in range(subs)], axis=0
        )

    def put_state(ref, j, value):
        if per:
            ref[j // per, pl.ds(pl.multiple_of((j % per) * modes, modes), modes)] = value
        else:
            count = modes // piece_rows
            for q in range(count):
                ref[j * count + q] = value[q * piece_rows : (q + 1) * piece_rows]

    def take_state(ref, j):
        if per:
            return ref[j // per, pl.ds(pl.multiple_of((j % per) * modes, modes), modes)]
        count = modes // piece_rows
        return jnp.concatenate([ref[j * count + q] for q in range(count)], axis=0)

    def rate_wide(j):
        return wide_s[j, :modes, :wide]

    def res_wide(j):
        return wide_s[j, modes:, :wide]

    def chan_rate(j):
        return wide_s[j, :modes, wide:]

    def signal_of(j):
        at = lanes(j)
        return key_ref[:, at].astype(F32) * value_ref[:, at].astype(F32)

    def strided(row, first):
        parts = []
        for h in range(wide // LANES):
            part = jnp.broadcast_to(row[:, h * LANES : (h + 1) * LANES], (SUB, LANES))
            parts.append(pltpu.roll(part, first, 1, stride=1, stride_axis=0))
        return jnp.concatenate(parts, axis=1)

    def batch(compute, store, js):
        results = [compute(j) for j in js]
        for j, result in zip(js, results):
            store(j, *result)

    def batches(compute, store, first, last, size):
        def step(i, _):
            batch(compute, store, [first + i * size + b for b in range(size)])
            return 0

        lax.fori_loop(0, (last - first) // size, step, 0)

    def transfer(source, target, phase, d, by_target=True):
        there = lax.rem(here + d, ctx_count)
        return pltpu.make_async_remote_copy(
            src_ref=source.at[there] if by_target else source,
            dst_ref=target.at[here],
            send_sem=send_sem.at[phase, d],
            recv_sem=recv_sem.at[phase, d],
            device_id={"ctx": there},
            device_id_type=MESH,
        )

    def all_others(act):
        def step(d, _):
            act(d)
            return 0

        lax.fori_loop(1, ctx_count, step, 0)

    def blocks_then_send(compute, store, source, target, phase):
        if per:
            def step(d, _):
                piece = lax.rem(here + d, ctx_count)
                batch(compute, store, [piece * per + b for b in range(per)])
                transfer(source, target, phase, d).start()
                return 0

            lax.fori_loop(1, ctx_count, step, 0)
            batch(compute, store, [here * per + b for b in range(per)])
        else:
            batches(compute, store, 0, blocks, 2)
            all_others(lambda d: transfer(source, target, phase, d).start())
        target[here] = source[here]

    def receive_then_blocks(compute, store, source, target, phase):
        target[here] = source[here]
        if per:
            batch(compute, store, [here * per + b for b in range(per)])

            def step(d, _):
                transfer(source, target, phase, d).wait_recv()
                piece = lax.rem(here - d + ctx_count, ctx_count)
                batch(compute, store, [piece * per + b for b in range(per)])
                return 0

            lax.fori_loop(1, ctx_count, step, 0)
        else:
            all_others(lambda d: transfer(source, target, phase, d).wait_recv())
            batches(compute, store, 0, blocks, 2)

    def owned_decay():
        if per:
            rates = jnp.concatenate([chan_rate(here * per + b) for b in range(per)], axis=0)
            return jnp.exp(-length * rates)
        count = modes // piece_rows
        whole = chan_rate(here // count)
        rates = whole[:piece_rows]
        for q in range(1, count):
            rates = jnp.where(
                here % count == q, whole[q * piece_rows : (q + 1) * piece_rows], rates
            )
        return jnp.exp(-length * rates)

    def join(own, source, target, result, phase, reverse):
        decay = owned_decay()
        all_others(lambda d: transfer(own, source, phase, d).wait_recv())

        def step(k, state):
            at = ctx_count - 1 - k if reverse else k
            target[at] = state
            return decay * state + source[at]

        lax.fori_loop(0, ctx_count, step, jnp.zeros((piece_rows, LANES), F32), unroll=True)
        all_others(lambda d: transfer(target, result, phase + 1, d).start())

    eye = unit(groups)
    tables = jnp.concatenate([jnp.exp(log_ref[...]), res_ref[...]], axis=0)
    rates, residues = transposed(tables[:modes], eye), transposed(tables[modes:], eye)
    spread_modes = (
        iota((modes, LANES), 0) == iota((modes, LANES), 1) % modes
    ).astype(F32).astype(BF16)
    own_row = iota((in_block, LANES), 0) == iota((in_block, LANES), 1) // modes
    widener = widen[...]
    for j in range(blocks):
        rolled = pltpu.roll(tables, (groups - j * in_block) % groups, 1)
        wide_s[j] = exact_dot(rolled, widener)
        rows = slice(j * in_block, (j + 1) * in_block)
        flat = exact_dot(jnp.concatenate([rates[rows], residues[rows]], axis=0), spread_modes)
        for q in range(2):
            part = jnp.where(own_row, flat[q * in_block : (q + 1) * in_block], 0.0)
            row_s[q, j : j + 1] = jnp.sum(part, axis=0, keepdims=True)

    row_id = iota((SUB, wide), 0)
    lane_id = iota((SUB, wide), 1) % SUB
    offset = (iota((modes, wide), 1) % SUB).astype(F32)
    time = iota((SUB, in_block * modes), 0).astype(F32)

    def states_of(j):
        ending = jnp.exp(-rate_wide(j) * (SUB - offset))
        table = jnp.concatenate([ending, ending * (SUB - offset)], axis=0)
        high, low = halves(signal_of(j))
        out = product(halves(table), (tokens_stack(high), tokens_stack(low)))
        step = jnp.exp(-chan_rate(j) * SUB)
        state = out[:modes, :LANES]
        for n in range(1, subs):
            state = step * state + out[:modes, n * LANES : (n + 1) * LANES]
        return out, state

    def states_put(j, out, state):
        sub_s[j] = out
        put_state(own_s, j, state)

    def local_of(j):
        taps = jnp.sum(
            res_wide(j) * jnp.exp(-rate_wide(j) * (SUB - 1.0 - offset)), axis=0, keepdims=True
        )
        toeplitz = jnp.where(lane_id <= row_id, strided(taps, LANES - SUB + 1), 0.0)
        signal = signal_of(j)
        high, low = halves(signal)
        out = product(halves(toeplitz), (tokens_stack(high), tokens_stack(low)))
        out = jnp.concatenate([out[:, n * LANES : (n + 1) * LANES] for n in range(subs)], axis=0)
        return (out + skip_ref[:, lanes(j)] * signal,)

    def local_put(j, out):
        mixed_s[:, lanes(j)] = out

    def carried_of(j):
        at = lanes(j)
        step = jnp.exp(-chan_rate(j) * SUB)
        state, moment = take_state(got_s, j), jnp.zeros((modes, LANES), F32)
        states, saved = [], []
        for n in range(subs):
            states.append(state)
            saved.append(jnp.concatenate([state, moment], axis=0))
            part = sub_s[j, :, n * LANES : (n + 1) * LANES]
            moment = step * (moment + SUB * state) + part[modes:]
            state = step * state + part[:modes]
        table = row_s[1, pl.ds(j, 1)] * jnp.exp(-row_s[0, pl.ds(j, 1)] * time)
        mixed = mixed_s[:, at] + carry_product(table, states)
        premix = gate_ref[:, at].astype(F32) * mixed
        pull = cot_ref[:, at].astype(F32) * gain_ref[:, at]
        return saved, moment, mixed, premix * premix, pull * premix

    def carried_put(j, saved, moment, mixed, square, inner):
        for n in range(subs):
            state_s[j, n] = saved[n]
        late_s[j] = moment
        mixed_s[:, lanes(j)] = mixed
        acc_s[0] += square
        acc_s[1] += inner

    pl.semaphore_wait(barrier, ctx_count - 1 + tp_count - 1)
    half = blocks // 2
    blocks_then_send(states_of, states_put, own_s, in_s, 0)
    batches(local_of, local_put, 0, half, 4)
    join(own_s, in_s, out_s, got_s, 0, False)
    batches(local_of, local_put, half, blocks, 4)
    receive_then_blocks(carried_of, carried_put, out_s, got_s, 1)

    for k in range(2):
        row = jnp.sum(acc_s[k].T, axis=0, keepdims=True)
        norm_own[4 * k : 4 * k + 4] = jnp.broadcast_to(row, (4, length))
    copies = []
    for d in range(1, tp_count):
        copy = pltpu.make_async_remote_copy(
            src_ref=norm_own,
            dst_ref=norm_got.at[side],
            send_sem=tp_send.at[d],
            recv_sem=tp_recv.at[d],
            device_id={"tp": lax.rem(side + d, tp_count)},
            device_id_type=MESH,
        )
        copy.start()
        copies.append(copy)
    norm_got[side] = norm_own[...]
    for copy in copies:
        copy.wait()
    sums = norm_got[0]
    for k in range(1, tp_count):
        sums = sums + norm_got[k]
    inverse_row = lax.rsqrt(sums[0:1] / full_width + EPSILON)
    inner_row = sums[4:5] * inverse_row / full_width
    acc_s[0] = jnp.broadcast_to(inverse_row, (LANES, length)).T
    acc_s[1] = jnp.broadcast_to(inner_row, (LANES, length)).T

    group_of_lane = iota((LANES, LANES), 0) // members
    group_of_wide = iota((wide, LANES), 0) // SUB
    lane_of = iota((LANES, LANES), 1)
    lane_of_wide = iota((wide, LANES), 1)
    half_row = iota((SUB, LANES), 0)

    def weight_of(j):
        at = lanes(j)
        inverse, inner = acc_s[0], acc_s[1]
        gate = gate_ref[:, at].astype(F32)
        normed = gate * mixed_s[:, at] * inverse
        dpre = (cot_ref[:, at].astype(F32) * gain_ref[:, at] - normed * inner) * inverse
        weight = dpre * gate
        start = jnp.exp(-rate_wide(j) * offset)
        table = jnp.concatenate([start, start * offset], axis=0)
        high, low = halves(weight)
        out = product(halves(table), (tokens_stack(high), tokens_stack(low)))
        step = jnp.exp(-chan_rate(j) * SUB)
        state = out[:modes, (subs - 1) * LANES :]
        for n in range(subs - 2, -1, -1):
            state = step * state + out[:modes, n * LANES : (n + 1) * LANES]
        return weight, out, state

    def weight_put(j, weight, out, state):
        weight_s[:, lanes(j)] = weight
        sub_s[j] = out
        put_state(own_b, j, state)

    def inside_of(j):
        at = lanes(j)
        inverse, inner = acc_s[0], acc_s[1]
        mixed = mixed_s[:, at]
        gain = gain_ref[:, at]
        normed = gate_ref[:, at].astype(F32) * mixed * inverse
        dpre = (cot_ref[:, at].astype(F32) * gain - normed * inner) * inverse
        weight = weight_s[:, at]
        start = jnp.exp(-rate_wide(j) * offset)
        taps = jnp.sum(res_wide(j) * start, axis=0, keepdims=True)
        toeplitz = jnp.where(lane_id >= row_id, strided(taps, 0), 0.0)
        high, low = halves(weight)
        right = (tokens_stack(high), tokens_stack(low))
        back = product(halves(toeplitz), right)
        back = jnp.concatenate([back[:, n * LANES : (n + 1) * LANES] for n in range(subs)], axis=0)

        left = tuple(
            jnp.concatenate([part[n * SUB : (n + 1) * SUB] for n in range(subs)], axis=1)
            for part in halves(signal_of(j))
        )
        pairs = jnp.where(lane_id >= row_id, product(left, right, dot_t), 0.0)
        lagged = []
        for h in range(wide // LANES):
            part = pairs[:, h * LANES : (h + 1) * LANES]
            bit = 1
            while bit < SUB:
                moved = pltpu.roll(part, LANES - bit, 1)
                part = jnp.where((half_row // bit) % 2 == 1, moved, part)
                bit *= 2
            lagged.append(jnp.sum(part, axis=0, keepdims=True))
        zeroth = start * jnp.concatenate(lagged, axis=1)
        local = jnp.concatenate([zeroth, zeroth * offset], axis=0)
        to_group = (group_of_wide + j * in_block == lane_of_wide).astype(F32).astype(BF16)
        total = exact_dot(local, to_group)

        cross = jnp.zeros((modes, LANES), F32)
        cross_moment = jnp.zeros((modes, LANES), F32)
        for n in range(subs):
            part = sub_s[j, :, n * LANES : (n + 1) * LANES]
            both = state_s[j, n]
            cross += part[:modes] * both[:modes]
            cross_moment += part[modes:] * both[:modes] + part[:modes] * both[modes:]
        to_group = (group_of_lane + j * in_block == lane_of).astype(F32).astype(BF16)
        total += exact_dot(jnp.concatenate([cross, cross_moment], axis=0), to_group)
        return (
            (normed * gain).astype(BF16),
            (dpre * mixed).astype(BF16),
            back + skip_ref[:, at] * weight,
            total,
        )

    def inside_put(j, mixer, grad_q, back, total):
        at = lanes(j)
        mixer_ref[:, at] = mixer
        gq_ref[:, at] = grad_q
        back_s[:, at] = back
        total_s[...] += total

    def ending_of(j):
        to_group = (group_of_lane + j * in_block == lane_of).astype(F32).astype(BF16)
        return (exact_dot(take_state(got_b, j) * late_s[j], to_group),)

    def ending_put(j, total):
        total_s[modes:] += total

    def signal_grad_of(j):
        at = lanes(j)
        step = jnp.exp(-chan_rate(j) * SUB)
        state = take_state(got_b, j)
        states = []
        for n in range(subs - 1, -1, -1):
            states.append(state)
            state = step * state + sub_s[j, :modes, n * LANES : (n + 1) * LANES]
        states.reverse()
        table = row_s[1, pl.ds(j, 1)] * jnp.exp(-row_s[0, pl.ds(j, 1)] * (SUB - time))
        grad = back_s[:, at] + carry_product(table, states)
        return (
            (grad * value_ref[:, at].astype(F32)).astype(BF16),
            (grad * key_ref[:, at].astype(F32)).astype(BF16),
        )

    def signal_grad_put(j, grad_k, grad_v):
        gk_ref[:, lanes(j)] = grad_k
        gv_ref[:, lanes(j)] = grad_v

    blocks_then_send(weight_of, weight_put, own_b, in_b, 2)
    batches(inside_of, inside_put, 0, half, 2)
    join(own_b, in_b, out_b, got_b, 2, True)
    batches(inside_of, inside_put, half, blocks, 2)
    receive_then_blocks(ending_of, ending_put, out_b, got_b, 3)

    part_s[...] = total_s[...]
    all_others(lambda d: transfer(part_s, part_got, 4, d, False).start())
    part_got[here] = part_s[...]
    batches(signal_grad_of, signal_grad_put, 0, blocks, 4)
    all_others(lambda d: transfer(part_s, part_got, 4, d, False).wait())
    sums = part_got[0]
    for k in range(1, ctx_count):
        sums = sums + part_got[k]
    filt_ref[...] = sums

    def drain(d):
        for phase, (source, target) in enumerate(
            ((own_s, in_s), (out_s, got_s), (own_b, in_b), (out_b, got_b))
        ):
            transfer(source, target, phase, d).wait_send()

    all_others(drain)


def finish(
    token_total, mixer_ref, gq_ref, gk_ref, gv_ref, filt_ref, res_ref, log_ref,
    mixer_out, gq_out, gk_out, gv_out, res_out, log_out, sems,
):
    pairs = ((mixer_ref, mixer_out), (gq_ref, gq_out), (gk_ref, gk_out), (gv_ref, gv_out))
    copies = [
        pltpu.make_async_copy(source, target, sems.at[k])
        for k, (source, target) in enumerate(pairs)
    ]
    for copy in copies:
        copy.start()
    modes = res_ref.shape[0]
    res_out[...] = filt_ref[:modes] / token_total
    log_out[...] = -res_ref[...] * jnp.exp(log_ref[...]) * filt_ref[modes:] / token_total
    for copy in copies:
        copy.wait()


def per_device(out_gate, key_proj, value_proj, residue, log_decay, skip, gain, cotangent):
    length, channels = out_gate.shape
    groups, modes = residue.shape
    members = channels // groups
    ctx_count, tp_count = lax.axis_size("ctx"), lax.axis_size("tp")
    blocks = channels // LANES
    in_block = LANES // members
    subs = length // SUB
    wide = in_block * SUB
    piece_rows = blocks * modes // ctx_count
    pieces = pltpu.VMEM((ctx_count, piece_rows, LANES), F32)
    wide_out = jax.ShapeDtypeStruct((length, channels), BF16)
    table_out = jax.ShapeDtypeStruct((modes, groups), F32)
    vmem = pl.BlockSpec(memory_space=pltpu.VMEM)
    anywhere = pl.BlockSpec(memory_space=pl.ANY)
    results = pl.pallas_call(
        functools.partial(kernel, ctx_count, tp_count, float(channels * tp_count)),
        out_shape=[wide_out] * 4 + [jax.ShapeDtypeStruct((2 * modes, groups), F32)],
        in_specs=[vmem] * 8,
        out_specs=[vmem] * 5,
        scratch_shapes=[
            pltpu.VMEM((length, channels), F32),
            pltpu.VMEM((length, channels), F32),
            pltpu.VMEM((length, channels), F32),
            pltpu.VMEM((blocks, 2 * modes, subs * LANES), F32),
            pltpu.VMEM((blocks, subs, 2 * modes, LANES), F32),
            pltpu.VMEM((blocks, modes, LANES), F32),
            pltpu.VMEM((wide, LANES), BF16),
            pltpu.VMEM((in_block * modes, LANES), BF16),
            pltpu.VMEM((groups, wide + LANES), BF16),
            pltpu.VMEM((blocks, 2 * modes, wide + LANES), F32),
            pltpu.VMEM((2, blocks, LANES), F32),
            pltpu.VMEM((2, length, LANES), F32),
            pltpu.VMEM((2 * modes, groups), F32),
            pieces, pieces, pieces, pieces,
            pieces, pieces, pieces, pieces,
            pltpu.VMEM((8, length), F32),
            pltpu.VMEM((tp_count, 8, length), F32),
            pltpu.VMEM((2 * modes, groups), F32),
            pltpu.VMEM((ctx_count, 2 * modes, groups), F32),
            pltpu.SemaphoreType.DMA((5, ctx_count)),
            pltpu.SemaphoreType.DMA((5, ctx_count)),
            pltpu.SemaphoreType.DMA((tp_count,)),
            pltpu.SemaphoreType.DMA((tp_count,)),
        ],
        compiler_params=pltpu.CompilerParams(
            collective_id=0, has_side_effects=True, vmem_limit_bytes=40 * 1024 * 1024
        ),
        name="mixer",
    )(out_gate, key_proj, value_proj, cotangent, skip[None], gain[None], residue.T, log_decay.T)
    *wide_results, grad_residue, grad_log_decay = pl.pallas_call(
        functools.partial(finish, float(length * ctx_count)),
        out_shape=[wide_out] * 4 + [table_out] * 2,
        in_specs=[vmem] * 7,
        out_specs=[anywhere] * 4 + [vmem] * 2,
        scratch_shapes=[pltpu.SemaphoreType.DMA((4,))],
        name="finish",
    )(*results, residue.T, log_decay.T)
    return *wide_results, grad_residue.T, grad_log_decay.T


def solution(mesh):
    wide, table, row = P("ctx", "tp"), P("tp", None), P("tp")
    return jax.shard_map(
        per_device,
        mesh=mesh,
        in_specs=(wide, wide, wide, table, table, row, row, wide),
        out_specs=(wide, wide, wide, wide, table, table),
        check_vma=False,
    )
```

time: 69.2 us -> 60.4 us (0.87)
  Pallas kernels: 56.7 us -> 48.5 us
  other arithmetic: 1.21 us -> 0 us
    pallas_call x1, Pallas kernels: 56.7 us -> 45 us  [per_device(): pl.pallas_call(functools.partial(kernel, ctx_count, tp_count, float(chann...]
    unnamed x21 -> x26, local copies, waits for them, and re-layouts: 4.6 us -> 10.8 us
    pallas_call x0 -> x1, Pallas kernels: none -> 3.48 us  [per_device(): pl.pallas_call(functools.partial(finish, float(length * ctx_count)), out_...]
    reshape x4 -> x0, local copies, waits for them, and re-layouts: 2.46 us -> none  [the longest x1 1.8 us: per_device(): res_wide = jnp.repeat(residue.T, SUB, axis=1)]
    broadcast_in_dim x3 -> x0, local copies, waits for them, and re-layouts: 1.95 us -> none  [the longest x1 1.3 us: per_device(): res_wide = jnp.repeat(residue.T, SUB, axis=1)]
    div x2 -> x0, other arithmetic: 1.21 us -> none  [the longest x1 0.61 us: per_device(): grad_log_decay = -residue * rate * filt[modes:].T / token_total]
    exp x2 -> x0, local copies, waits for them, and re-layouts: 0.81 us -> none  [per_device(): rate = jnp.exp(log_decay)]
where the time goes in v2:
time: 60.4 us; the launch traced here: 59.9 us
  Pallas kernels  48.5 us (80%)
  local copies, waits for them, and re-layouts  10.8 us (18%)
  between operations  0.67 us (1%)
    pallas_call x1, Pallas kernels, per_device(): pl.pallas_call(functools.partial(kernel, ctx_count, tp_count, float(chann...  45 us
    unnamed x26, local copies, waits for them, and re-layouts  10.8 us
    pallas_call x1, Pallas kernels, per_device(): pl.pallas_call(functools.partial(finish, float(length * ctx_count)), out_...  3.48 us

profile of v2, /device:TPU:0, one launch (start us, length us, event | category | flops | bytes accessed | tf_op | source)
XLA Modules:
  0.0 59.9 jit_solution(13291684475274159161)
XLA Ops:
  0.6 0.0 copy-start
  0.6 1.0 %copy-done = bf16[128,2048]{1,0:T(8,128)(2,1)S(1)} copy-done((bf16[128,2048]{1,0:T(8,128)(2,1)S(1)}, bf16[128,2048]{1,0:T(8,128)(2,1)}, u32[]{:S(2)}) %copy-start) | copy-done | bytes 524312
  1.7 0.0 copy-start.1
  1.7 1.0 %copy-done.1 = bf16[128,2048]{1,0:T(8,128)(2,1)S(1)} copy-done((bf16[128,2048]{1,0:T(8,128)(2,1)S(1)}, bf16[128,2048]{1,0:T(8,128)(2,1)}, u32[]{:S(2)}) %copy-start.1) | copy-done | bytes 524312
  2.7 0.0 copy-start.2
  2.7 1.0 %copy-done.2 = bf16[128,2048]{1,0:T(8,128)(2,1)S(1)} copy-done((bf16[128,2048]{1,0:T(8,128)(2,1)S(1)}, bf16[128,2048]{1,0:T(8,128)(2,1)}, u32[]{:S(2)}) %copy-start.2) | copy-done | bytes 524312
  3.8 0.0 copy-start.3
  3.8 1.0 %copy-done.3 = bf16[128,2048]{1,0:T(8,128)(2,1)S(1)} copy-done((bf16[128,2048]{1,0:T(8,128)(2,1)S(1)}, bf16[128,2048]{1,0:T(8,128)(2,1)}, u32[]{:S(2)}) %copy-start.3) | copy-done | bytes 524312
  4.8 0.0 copy-start.8
  4.8 0.7 %copy-done.8 = f32[128,16]{0,1:T(8,128)S(1)} copy-done((f32[128,16]{0,1:T(8,128)S(1)}, f32[128,16]{0,1:T(8,128)}, u32[]{:S(2)}) %copy-start.8) | copy-done | bytes 8216
  5.5 0.0 copy-start.9
  5.5 0.7 %copy-done.9 = f32[128,16]{0,1:T(8,128)S(1)} copy-done((f32[128,16]{0,1:T(8,128)S(1)}, f32[128,16]{0,1:T(8,128)}, u32[]{:S(2)}) %copy-start.9) | copy-done | bytes 8216
  6.2 0.0 copy-start.11
  6.2 0.7 %copy-done.11 = f32[2048]{0:T(1024)S(1)} copy-done((f32[2048]{0:T(1024)S(1)}, f32[2048]{0:T(1024)}, u32[]{:S(2)}) %copy-start.11) | copy-done | bytes 8216
  6.9 0.0 copy-start.12
  6.9 0.7 %copy-done.12 = f32[2048]{0:T(1024)S(1)} copy-done((f32[2048]{0:T(1024)S(1)}, f32[2048]{0:T(1024)}, u32[]{:S(2)}) %copy-start.12) | copy-done | bytes 8216
  7.6 45.0 %mixer.1 = (bf16[128,2048]{1,0:T(8,128)(2,1)S(1)}, bf16[128,2048]{1,0:T(8,128)(2,1)S(1)}, bf16[128,2048]{1,0:T(8,128)(2,1)S(1)}, bf16[128,2048]{1,0:T(8,128)(2,1)S(1)}, f32[32,128]{1,0:T(8,128)S(1)}) custom-call(bf16[128,2048]{1,0:T(8,128)(2,1)S(1)} %copy-done, bf16[128,2048]{1,0:T(8,128)(2,1)S(1)} %copy-done.1, bf16[128,2048]{1,0:T(8,128)(2,1)S(1)} %copy-done.2, ...), custom_call_target="tpu_custom_call" | custom-call | tf_op jit(solution)/shard_map/mixer/pallas_call | solution.py:570
  52.6 0.0 copy-start.4
  52.6 0.8 %copy-done.4 = bf16[128,2048]{1,0:T(8,128)(2,1)} copy-done((bf16[128,2048]{1,0:T(8,128)(2,1)}, bf16[128,2048]{1,0:T(8,128)(2,1)S(1)}, u32[]{:S(2)}) %copy-start.4) | copy-done | bytes 524312
  53.4 0.8 %copy-done.5 = bf16[128,2048]{1,0:T(8,128)(2,1)} copy-done((bf16[128,2048]{1,0:T(8,128)(2,1)}, bf16[128,2048]{1,0:T(8,128)(2,1)S(1)}, u32[]{:S(2)}) %copy-start.5) | copy-done | bytes 524312
  54.2 0.8 %copy-done.6 = bf16[128,2048]{1,0:T(8,128)(2,1)} copy-done((bf16[128,2048]{1,0:T(8,128)(2,1)}, bf16[128,2048]{1,0:T(8,128)(2,1)S(1)}, u32[]{:S(2)}) %copy-start.6) | copy-done | bytes 524312
  55.0 0.8 %copy-done.7 = bf16[128,2048]{1,0:T(8,128)(2,1)} copy-done((bf16[128,2048]{1,0:T(8,128)(2,1)}, bf16[128,2048]{1,0:T(8,128)(2,1)S(1)}, u32[]{:S(2)}) %copy-start.7) | copy-done | bytes 524312
  55.8 0.6 copy-done.10
  56.4 3.5 %finish.1 = (bf16[128,2048]{1,0:T(8,128)(2,1)}, bf16[128,2048]{1,0:T(8,128)(2,1)}, bf16[128,2048]{1,0:T(8,128)(2,1)}, bf16[128,2048]{1,0:T(8,128)(2,1)}, f32[16,128]{1,0:T(8,128)}, /*index=5*/f32[16,128]{1,0:T(8,128)}) custom-call(bf16[128,2048]{1,0:T(8,128)(2,1)} %copy-done.4, bf16[128,2048]{1,0:T(8,128)(2,1)} %copy-done.5, bf16[128,2048]{1,0:T(8,128)(2,1)} %copy-done.6, ...), custom_call_target="tpu_custom_call" | custom-call | tf_op jit(solution)/shard_map/finish/pallas_call | solution.py:605
  (4 shorter events, 0.0 us)
Async XLA Ops:
  0.6 1.0 %copy-start = (bf16[128,2048]{1,0:T(8,128)(2,1)S(1)}, bf16[128,2048]{1,0:T(8,128)(2,1)}, u32[]{:S(2)}) copy-start(bf16[128,2048]{1,0:T(8,128)(2,1)} %gate_ref.1) | copy-start | bytes 1572868
  1.7 1.0 %copy-start.1 = (bf16[128,2048]{1,0:T(8,128)(2,1)S(1)}, bf16[128,2048]{1,0:T(8,128)(2,1)}, u32[]{:S(2)}) copy-start(bf16[128,2048]{1,0:T(8,128)(2,1)} %key_ref.1) | copy-start | bytes 1572868
  2.7 1.0 %copy-start.2 = (bf16[128,2048]{1,0:T(8,128)(2,1)S(1)}, bf16[128,2048]{1,0:T(8,128)(2,1)}, u32[]{:S(2)}) copy-start(bf16[128,2048]{1,0:T(8,128)(2,1)} %value_ref.1) | copy-start | bytes 1572868
  3.8 1.0 %copy-start.3 = (bf16[128,2048]{1,0:T(8,128)(2,1)S(1)}, bf16[128,2048]{1,0:T(8,128)(2,1)}, u32[]{:S(2)}) copy-start(bf16[128,2048]{1,0:T(8,128)(2,1)} %cot_ref.1) | copy-start | bytes 1572868
  4.8 0.7 %copy-start.8 = (f32[128,16]{0,1:T(8,128)S(1)}, f32[128,16]{0,1:T(8,128)}, u32[]{:S(2)}) copy-start(f32[128,16]{0,1:T(8,128)} %param.11) | copy-start | bytes 24580
  5.5 0.7 %copy-start.9 = (f32[128,16]{0,1:T(8,128)S(1)}, f32[128,16]{0,1:T(8,128)}, u32[]{:S(2)}) copy-start(f32[128,16]{0,1:T(8,128)} %param.12) | copy-start | bytes 24580
  6.2 0.7 %copy-start.11 = (f32[2048]{0:T(1024)S(1)}, f32[2048]{0:T(1024)}, u32[]{:S(2)}) copy-start(f32[2048]{0:T(1024)} %param.13) | copy-start | bytes 24580
  6.9 0.7 %copy-start.12 = (f32[2048]{0:T(1024)S(1)}, f32[2048]{0:T(1024)}, u32[]{:S(2)}) copy-start(f32[2048]{0:T(1024)} %param.14) | copy-start | bytes 24580
  52.6 0.8 %copy-start.4 = (bf16[128,2048]{1,0:T(8,128)(2,1)}, bf16[128,2048]{1,0:T(8,128)(2,1)S(1)}, u32[]{:S(2)}) copy-start(bf16[128,2048]{1,0:T(8,128)(2,1)S(1)} %get-tuple-element.17.mixer_ref) | copy-start | bytes 1572868
  53.4 0.8 %copy-start.5 = (bf16[128,2048]{1,0:T(8,128)(2,1)}, bf16[128,2048]{1,0:T(8,128)(2,1)S(1)}, u32[]{:S(2)}) copy-start(bf16[128,2048]{1,0:T(8,128)(2,1)S(1)} %get-tuple-element.18.gq_ref) | copy-start | bytes 1572868
  54.2 0.8 %copy-start.6 = (bf16[128,2048]{1,0:T(8,128)(2,1)}, bf16[128,2048]{1,0:T(8,128)(2,1)S(1)}, u32[]{:S(2)}) copy-start(bf16[128,2048]{1,0:T(8,128)(2,1)S(1)} %get-tuple-element.19.gk_ref) | copy-start | bytes 1572868
  55.0 0.8 %copy-start.7 = (bf16[128,2048]{1,0:T(8,128)(2,1)}, bf16[128,2048]{1,0:T(8,128)(2,1)S(1)}, u32[]{:S(2)}) copy-start(bf16[128,2048]{1,0:T(8,128)(2,1)S(1)} %get-tuple-element.20.gv_ref) | copy-start | bytes 1572868
  55.8 0.6 copy-start.10

commit v3 on v2

--- a/solution.py
+++ b/solution.py
@@ -64,6 +64,20 @@
     ctx_count,
     tp_count,
     full_width,
+    gate_in,
+    key_in,
+    value_in,
+    cot_in,
+    skip_in,
+    gain_in,
+    res_in,
+    log_in,
+    mixer_out,
+    gq_out,
+    gk_out,
+    gv_out,
+    res_out,
+    log_out,
     gate_ref,
     key_ref,
     value_ref,
@@ -87,9 +101,12 @@
     mask_mode,
     widen,
     wide_s,
+    table_s,
+    toeplitz_s,
+    local_s,
+    cross_s,
     row_s,
     acc_s,
-    total_s,
     own_s,
     in_s,
     out_s,
@@ -106,6 +123,9 @@
     recv_sem,
     tp_send,
     tp_recv,
+    load_sem,
+    store_sem,
+    part_sem,
 ):
     here = lax.axis_index("ctx")
     side = lax.axis_index("tp")
@@ -119,6 +139,24 @@
     piece_rows = blocks * modes // ctx_count
     per = piece_rows // modes
 
+    loads = [
+        pltpu.make_async_copy(source, target, load_sem.at[k])
+        for k, (source, target) in enumerate(
+            (
+                (res_in, res_ref),
+                (log_in, log_ref),
+                (key_in, key_ref),
+                (value_in, value_ref),
+                (skip_in, skip_ref),
+                (gate_in, gate_ref),
+                (cot_in, cot_ref),
+                (gain_in, gain_ref),
+            )
+        )
+    ]
+    for load in loads:
+        load.start()
+
     barrier = pltpu.get_barrier_semaphore()
     for d in range(1, ctx_count):
         pl.semaphore_signal(
@@ -140,7 +178,6 @@
         iota((groups, LANES), 0) == iota((groups, LANES), 1) // members
     ).astype(F32).astype(BF16)
     acc_s[...] = jnp.zeros_like(acc_s)
-    total_s[...] = jnp.zeros_like(total_s)
 
     def lanes(j, width=LANES):
         return pl.ds(pl.multiple_of(j * width, width), width)
@@ -287,20 +324,23 @@
         all_others(lambda d: transfer(target, result, phase + 1, d).start())
 
     eye = unit(groups)
+    for load in loads[:2]:
+        load.wait()
     tables = jnp.concatenate([jnp.exp(log_ref[...]), res_ref[...]], axis=0)
     rates, residues = transposed(tables[:modes], eye), transposed(tables[modes:], eye)
     spread_modes = (
         iota((modes, LANES), 0) == iota((modes, LANES), 1) % modes
     ).astype(F32).astype(BF16)
     own_row = iota((in_block, LANES), 0) == iota((in_block, LANES), 1) // modes
-    widener = widen[...]
-    for j in range(blocks):
-        rolled = pltpu.roll(tables, (groups - j * in_block) % groups, 1)
-        wide_s[j] = exact_dot(rolled, widener)
-        rows = slice(j * in_block, (j + 1) * in_block)
-        flat = exact_dot(jnp.concatenate([rates[rows], residues[rows]], axis=0), spread_modes)
-        for q in range(2):
-            part = jnp.where(own_row, flat[q * in_block : (q + 1) * in_block], 0.0)
+    rolled = [
+        pltpu.roll(tables, (groups - j * in_block) % groups, 1) for j in range(blocks)
+    ]
+    wide_s[...] = exact_dot(jnp.concatenate(rolled, axis=0), widen[...]).reshape(wide_s.shape)
+    flat = exact_dot(jnp.concatenate([rates, residues], axis=0), spread_modes)
+    for q in range(2):
+        for j in range(blocks):
+            first = q * groups + j * in_block
+            part = jnp.where(own_row, flat[first : first + in_block], 0.0)
             row_s[q, j : j + 1] = jnp.sum(part, axis=0, keepdims=True)
 
     row_id = iota((SUB, wide), 0)
@@ -362,12 +402,17 @@
         acc_s[0] += square
         acc_s[1] += inner
 
+    for load in loads[2:4]:
+        load.wait()
     pl.semaphore_wait(barrier, ctx_count - 1 + tp_count - 1)
     half = blocks // 2
     blocks_then_send(states_of, states_put, own_s, in_s, 0)
+    loads[4].wait()
     batches(local_of, local_put, 0, half, 4)
     join(own_s, in_s, out_s, got_s, 0, False)
     batches(local_of, local_put, half, blocks, 4)
+    for load in loads[5:]:
+        load.wait()
     receive_then_blocks(carried_of, carried_put, out_s, got_s, 1)
 
     for k in range(2):
@@ -386,6 +431,18 @@
         copy.start()
         copies.append(copy)
     norm_got[side] = norm_own[...]
+
+    def tables_of(j):
+        start = jnp.exp(-rate_wide(j) * offset)
+        taps = jnp.sum(res_wide(j) * start, axis=0, keepdims=True)
+        toeplitz = jnp.where(lane_id >= row_id, strided(taps, 0), 0.0)
+        return halves(jnp.concatenate([start, start * offset], axis=0)) + halves(toeplitz)
+
+    def tables_put(j, high, low, toeplitz_high, toeplitz_low):
+        table_s[j, 0], table_s[j, 1] = high, low
+        toeplitz_s[j, 0], toeplitz_s[j, 1] = toeplitz_high, toeplitz_low
+
+    batches(tables_of, tables_put, 0, blocks, 4)
     for copy in copies:
         copy.wait()
     sums = norm_got[0]
@@ -396,10 +453,12 @@
     acc_s[0] = jnp.broadcast_to(inverse_row, (LANES, length)).T
     acc_s[1] = jnp.broadcast_to(inner_row, (LANES, length)).T
 
-    group_of_lane = iota((LANES, LANES), 0) // members
-    group_of_wide = iota((wide, LANES), 0) // SUB
-    lane_of = iota((LANES, LANES), 1)
-    lane_of_wide = iota((wide, LANES), 1)
+    to_group = (
+        iota((LANES, groups), 0) // members == iota((LANES, groups), 1)
+    ).astype(F32).astype(BF16)
+    wide_to_group = (
+        iota((wide, groups), 0) // SUB == iota((wide, groups), 1)
+    ).astype(F32).astype(BF16)
     half_row = iota((SUB, LANES), 0)
 
     def weight_of(j):
@@ -409,10 +468,8 @@
         normed = gate * mixed_s[:, at] * inverse
         dpre = (cot_ref[:, at].astype(F32) * gain_ref[:, at] - normed * inner) * inverse
         weight = dpre * gate
-        start = jnp.exp(-rate_wide(j) * offset)
-        table = jnp.concatenate([start, start * offset], axis=0)
         high, low = halves(weight)
-        out = product(halves(table), (tokens_stack(high), tokens_stack(low)))
+        out = product((table_s[j, 0], table_s[j, 1]), (tokens_stack(high), tokens_stack(low)))
         step = jnp.exp(-chan_rate(j) * SUB)
         state = out[:modes, (subs - 1) * LANES :]
         for n in range(subs - 2, -1, -1):
@@ -433,11 +490,9 @@
         dpre = (cot_ref[:, at].astype(F32) * gain - normed * inner) * inverse
         weight = weight_s[:, at]
         start = jnp.exp(-rate_wide(j) * offset)
-        taps = jnp.sum(res_wide(j) * start, axis=0, keepdims=True)
-        toeplitz = jnp.where(lane_id >= row_id, strided(taps, 0), 0.0)
         high, low = halves(weight)
         right = (tokens_stack(high), tokens_stack(low))
-        back = product(halves(toeplitz), right)
+        back = product((toeplitz_s[j, 0], toeplitz_s[j, 1]), right)
         back = jnp.concatenate([back[:, n * LANES : (n + 1) * LANES] for n in range(subs)], axis=0)
 
         left = tuple(
@@ -456,8 +511,6 @@
             lagged.append(jnp.sum(part, axis=0, keepdims=True))
         zeroth = start * jnp.concatenate(lagged, axis=1)
         local = jnp.concatenate([zeroth, zeroth * offset], axis=0)
-        to_group = (group_of_wide + j * in_block == lane_of_wide).astype(F32).astype(BF16)
-        total = exact_dot(local, to_group)
 
         cross = jnp.zeros((modes, LANES), F32)
         cross_moment = jnp.zeros((modes, LANES), F32)
@@ -466,28 +519,34 @@
             both = state_s[j, n]
             cross += part[:modes] * both[:modes]
             cross_moment += part[modes:] * both[:modes] + part[:modes] * both[modes:]
-        to_group = (group_of_lane + j * in_block == lane_of).astype(F32).astype(BF16)
-        total += exact_dot(jnp.concatenate([cross, cross_moment], axis=0), to_group)
         return (
             (normed * gain).astype(BF16),
             (dpre * mixed).astype(BF16),
             back + skip_ref[:, at] * weight,
-            total,
-        )
-
-    def inside_put(j, mixer, grad_q, back, total):
+            local,
+            jnp.concatenate([cross, cross_moment], axis=0),
+        )
+
+    def inside_put(j, mixer, grad_q, back, local, cross):
         at = lanes(j)
         mixer_ref[:, at] = mixer
         gq_ref[:, at] = grad_q
         back_s[:, at] = back
-        total_s[...] += total
+        local_s[j] = local
+        cross_s[j] = cross
 
     def ending_of(j):
-        to_group = (group_of_lane + j * in_block == lane_of).astype(F32).astype(BF16)
-        return (exact_dot(take_state(got_b, j) * late_s[j], to_group),)
-
-    def ending_put(j, total):
-        total_s[modes:] += total
+        return (cross_s[j, modes:] + take_state(got_b, j) * late_s[j],)
+
+    def ending_put(j, moment):
+        cross_s[j, modes:] = moment
+
+    def group_sums(ref, ones):
+        rows = exact_dot(ref[...].reshape(blocks * 2 * modes, ref.shape[2]), ones)
+        total = rows[: 2 * modes]
+        for j in range(1, blocks):
+            total += pltpu.roll(rows[2 * modes * j : 2 * modes * (j + 1)], j * in_block, 1)
+        return total
 
     def signal_grad_of(j):
         at = lanes(j)
@@ -513,17 +572,47 @@
     batches(inside_of, inside_put, 0, half, 2)
     join(own_b, in_b, out_b, got_b, 2, True)
     batches(inside_of, inside_put, half, blocks, 2)
+    stores = [
+        pltpu.make_async_copy(mixer_ref, mixer_out, store_sem.at[0]),
+        pltpu.make_async_copy(gq_ref, gq_out, store_sem.at[1]),
+    ]
+    for store in stores:
+        store.start()
+    inside_total = group_sums(local_s, wide_to_group)
     receive_then_blocks(ending_of, ending_put, out_b, got_b, 3)
-
-    part_s[...] = total_s[...]
+    part_s[...] = inside_total + group_sums(cross_s, to_group)
     all_others(lambda d: transfer(part_s, part_got, 4, d, False).start())
     part_got[here] = part_s[...]
-    batches(signal_grad_of, signal_grad_put, 0, blocks, 4)
+
+    size = 4
+
+    def grad_stores(i):
+        at = lanes(i, size * LANES)
+        return [
+            pltpu.make_async_copy(source.at[:, at], target.at[:, at], part_sem.at[k, i])
+            for k, (source, target) in enumerate(((gk_ref, gk_out), (gv_ref, gv_out)))
+        ]
+
+    def grads(i, _):
+        batch(signal_grad_of, signal_grad_put, [i * size + b for b in range(size)])
+        for store in grad_stores(i):
+            store.start()
+        return 0
+
+    lax.fori_loop(0, blocks // size, grads, 0)
     all_others(lambda d: transfer(part_s, part_got, 4, d, False).wait())
     sums = part_got[0]
     for k in range(1, ctx_count):
         sums = sums + part_got[k]
-    filt_ref[...] = sums
+    scale = 1.0 / (length * ctx_count)
+    filt_ref[:modes] = sums[:modes] * scale
+    filt_ref[modes:] = -res_ref[...] * jnp.exp(log_ref[...]) * sums[modes:] * scale
+    last = [
+        pltpu.make_async_copy(filt_ref.at[:modes], res_out, store_sem.at[2]),
+        pltpu.make_async_copy(filt_ref.at[modes:], log_out, store_sem.at[3]),
+    ]
+    for store in last:
+        store.start()
 
     def drain(d):
         for phase, (source, target) in enumerate(
@@ -532,22 +621,20 @@
             transfer(source, target, phase, d).wait_send()
 
     all_others(drain)
-
-
-def finish(
-    token_total, mixer_ref, gq_ref, gk_ref, gv_ref, filt_ref, res_ref, log_ref,
-    mixer_out, gq_out, gk_out, gv_out, res_out, log_out, sems,
-):
-    pairs = ((mixer_ref, mixer_out), (gq_ref, gq_out), (gk_ref, gk_out), (gv_ref, gv_out))
+    for i in range(blocks // size):
+        stores += grad_stores(i)
+    for store in stores + last:
+        store.wait()
+
+
+def finish(*refs):
+    sources, targets, sems = refs[:6], refs[6:12], refs[12]
     copies = [
         pltpu.make_async_copy(source, target, sems.at[k])
-        for k, (source, target) in enumerate(pairs)
+        for k, (source, target) in enumerate(zip(sources, targets))
     ]
     for copy in copies:
         copy.start()
-    modes = res_ref.shape[0]
-    res_out[...] = filt_ref[:modes] / token_total
-    log_out[...] = -res_ref[...] * jnp.exp(log_ref[...]) * filt_ref[modes:] / token_total
     for copy in copies:
         copy.wait()
 
@@ -565,14 +652,27 @@
     pieces = pltpu.VMEM((ctx_count, piece_rows, LANES), F32)
     wide_out = jax.ShapeDtypeStruct((length, channels), BF16)
     table_out = jax.ShapeDtypeStruct((modes, groups), F32)
-    vmem = pl.BlockSpec(memory_space=pltpu.VMEM)
-    anywhere = pl.BlockSpec(memory_space=pl.ANY)
-    results = pl.pallas_call(
+    hbm = pl.BlockSpec(memory_space=pltpu.HBM)
+    results = [wide_out] * 4 + [table_out] * 2
+    computed = pl.pallas_call(
         functools.partial(kernel, ctx_count, tp_count, float(channels * tp_count)),
-        out_shape=[wide_out] * 4 + [jax.ShapeDtypeStruct((2 * modes, groups), F32)],
-        in_specs=[vmem] * 8,
-        out_specs=[vmem] * 5,
+        out_shape=results,
+        in_specs=[hbm] * 8,
+        out_specs=[hbm] * 6,
         scratch_shapes=[
+            pltpu.VMEM((length, channels), BF16),
+            pltpu.VMEM((length, channels), BF16),
+            pltpu.VMEM((length, channels), BF16),
+            pltpu.VMEM((length, channels), BF16),
+            pltpu.VMEM((1, channels), F32),
+            pltpu.VMEM((1, channels), F32),
+            pltpu.VMEM((modes, groups), F32),
+            pltpu.VMEM((modes, groups), F32),
+            pltpu.VMEM((length, channels), BF16),
+            pltpu.VMEM((length, channels), BF16),
+            pltpu.VMEM((length, channels), BF16),
+            pltpu.VMEM((length, channels), BF16),
+            pltpu.VMEM((2 * modes, groups), F32),
             pltpu.VMEM((length, channels), F32),
             pltpu.VMEM((length, channels), F32),
             pltpu.VMEM((length, channels), F32),
@@ -583,9 +683,12 @@
             pltpu.VMEM((in_block * modes, LANES), BF16),
             pltpu.VMEM((groups, wide + LANES), BF16),
             pltpu.VMEM((blocks, 2 * modes, wide + LANES), F32),
+            pltpu.VMEM((blocks, 2, 2 * modes, wide), BF16),
+            pltpu.VMEM((blocks, 2, SUB, wide), BF16),
+            pltpu.VMEM((blocks, 2 * modes, wide), F32),
+            pltpu.VMEM((blocks, 2 * modes, LANES), F32),
             pltpu.VMEM((2, blocks, LANES), F32),
             pltpu.VMEM((2, length, LANES), F32),
-            pltpu.VMEM((2 * modes, groups), F32),
             pieces, pieces, pieces, pieces,
             pieces, pieces, pieces, pieces,
             pltpu.VMEM((8, length), F32),
@@ -596,20 +699,24 @@
             pltpu.SemaphoreType.DMA((5, ctx_count)),
             pltpu.SemaphoreType.DMA((tp_count,)),
             pltpu.SemaphoreType.DMA((tp_count,)),
+            pltpu.SemaphoreType.DMA((8,)),
+            pltpu.SemaphoreType.DMA((4,)),
+            pltpu.SemaphoreType.DMA((2, blocks)),
         ],
         compiler_params=pltpu.CompilerParams(
-            collective_id=0, has_side_effects=True, vmem_limit_bytes=40 * 1024 * 1024
+            collective_id=0, has_side_effects=True, vmem_limit_bytes=60 * 1024 * 1024
         ),
         name="mixer",
     )(out_gate, key_proj, value_proj, cotangent, skip[None], gain[None], residue.T, log_decay.T)
     *wide_results, grad_residue, grad_log_decay = pl.pallas_call(
-        functools.partial(finish, float(length * ctx_count)),
-        out_shape=[wide_out] * 4 + [table_out] * 2,
-        in_specs=[vmem] * 7,
-        out_specs=[anywhere] * 4 + [vmem] * 2,
-        scratch_shapes=[pltpu.SemaphoreType.DMA((4,))],
+        finish,
+        out_shape=results,
+        in_specs=[hbm] * 6,
+        out_specs=[hbm] * 6,
+        scratch_shapes=[pltpu.SemaphoreType.DMA((6,))],
+        compiler_params=pltpu.CompilerParams(vmem_limit_bytes=60 * 1024 * 1024),
         name="finish",
-    )(*results, residue.T, log_decay.T)
+    )(*computed)
     return *wide_results, grad_residue.T, grad_log_decay.T
 
 

time: 60.4 us -> 106 us (1.75)
  Pallas kernels: 48.5 us -> 105 us
  local copies, waits for them, and re-layouts: 10.8 us -> 0 us
    pallas_call x1, Pallas kernels: 3.48 us -> 65.2 us  [per_device(): pl.pallas_call(finish, out_shape=results, in_specs=[hbm] * 6, out_specs=[...]
    unnamed x26 -> x0, local copies, waits for them, and re-layouts: 10.8 us -> none
    pallas_call x1, Pallas kernels: 45 us -> 39.9 us  [per_device(): pl.pallas_call(functools.partial(kernel, ctx_count, tp_count, float(chann...]
where the time goes in v3:
time: 106 us
  Pallas kernels  105 us (99%)
    pallas_call x1, Pallas kernels, per_device(): pl.pallas_call(finish, out_shape=results, in_specs=[hbm] * 6, out_specs=[...  65.2 us
    pallas_call x1, Pallas kernels, per_device(): pl.pallas_call(functools.partial(kernel, ctx_count, tp_count, float(chann...  39.9 us

profile of v3, /device:TPU:0, one launch (start us, length us, event | category | flops | bytes accessed | tf_op | source)
XLA Modules:
  0.0 105.7 jit_solution(17448462055569870995)
XLA Ops:
  0.6 39.9 %mixer.1 = (bf16[128,2048]{1,0:T(8,128)(2,1)}, bf16[128,2048]{1,0:T(8,128)(2,1)}, bf16[128,2048]{1,0:T(8,128)(2,1)}, bf16[128,2048]{1,0:T(8,128)(2,1)}, f32[16,128]{1,0:T(8,128)}, /*index=5*/f32[16,128]{1,0:T(8,128)}) custom-call(bf16[128,2048]{1,0:T(8,128)(2,1)} %gate_in.1, bf16[128,2048]{1,0:T(8,128)(2,1)} %key_in.1, bf16[128,2048]{1,0:T(8,128)(2,1)} %value_in.1, ...), custom_call_target="tpu_custom_call" | custom-call | tf_op jit(solution)/shard_map/mixer/pallas_call | solution.py:657
  40.5 65.2 %finish.1 = (bf16[128,2048]{1,0:T(8,128)(2,1)}, bf16[128,2048]{1,0:T(8,128)(2,1)}, bf16[128,2048]{1,0:T(8,128)(2,1)}, bf16[128,2048]{1,0:T(8,128)(2,1)}, f32[16,128]{1,0:T(8,128)}, /*index=5*/f32[16,128]{1,0:T(8,128)}) custom-call(bf16[128,2048]{1,0:T(8,128)(2,1)} %get-tuple-element.18.refs_0_, bf16[128,2048]{1,0:T(8,128)(2,1)} %get-tuple-element.19.refs_1_, ...), custom_call_target="tpu_custom_call" | custom-call | tf_op jit(solution)/shard_map/finish/pallas_call | solution.py:711

commit v4 on v3

--- a/solution.py
+++ b/solution.py
@@ -10,6 +10,7 @@
 EPSILON = 1e-06
 LANES = 128
 SUB = 32
+PART_ROWS = 64
 F32 = jnp.float32
 BF16 = jnp.bfloat16
 MESH = pl.DeviceIdType.MESH
@@ -103,6 +104,7 @@
     wide_s,
     table_s,
     toeplitz_s,
+    turned_s,
     local_s,
     cross_s,
     row_s,
@@ -267,16 +269,32 @@
 
         lax.fori_loop(1, ctx_count, step, 0)
 
+    pair = 2 if ctx_count % 2 == 0 else 1
+
+    def piece_blocks(piece):
+        return [piece * per + b for b in range(per)]
+
     def blocks_then_send(compute, store, source, target, phase):
         if per:
-            def step(d, _):
-                piece = lax.rem(here + d, ctx_count)
-                batch(compute, store, [piece * per + b for b in range(per)])
-                transfer(source, target, phase, d).start()
+            def step(i, _):
+                first = i * pair + 1
+                batch(
+                    compute,
+                    store,
+                    [
+                        j
+                        for b in range(pair)
+                        for j in piece_blocks(lax.rem(here + first + b, ctx_count))
+                    ],
+                )
+                for b in range(pair):
+                    @pl.when(first + b < ctx_count)
+                    def _():
+                        transfer(source, target, phase, first + b).start()
+
                 return 0
 
-            lax.fori_loop(1, ctx_count, step, 0)
-            batch(compute, store, [here * per + b for b in range(per)])
+            lax.fori_loop(0, ctx_count // pair, step, 0)
         else:
             batches(compute, store, 0, blocks, 2)
             all_others(lambda d: transfer(source, target, phase, d).start())
@@ -285,15 +303,25 @@
     def receive_then_blocks(compute, store, source, target, phase):
         target[here] = source[here]
         if per:
-            batch(compute, store, [here * per + b for b in range(per)])
-
-            def step(d, _):
-                transfer(source, target, phase, d).wait_recv()
-                piece = lax.rem(here - d + ctx_count, ctx_count)
-                batch(compute, store, [piece * per + b for b in range(per)])
+            def step(i, _):
+                first = i * pair
+                for b in range(pair):
+                    @pl.when(first + b > 0)
+                    def _():
+                        transfer(source, target, phase, first + b).wait_recv()
+
+                batch(
+                    compute,
+                    store,
+                    [
+                        j
+                        for b in range(pair)
+                        for j in piece_blocks(lax.rem(here - first - b + ctx_count, ctx_count))
+                    ],
+                )
                 return 0
 
-            lax.fori_loop(1, ctx_count, step, 0)
+            lax.fori_loop(0, ctx_count // pair, step, 0)
         else:
             all_others(lambda d: transfer(source, target, phase, d).wait_recv())
             batches(compute, store, 0, blocks, 2)
@@ -432,13 +460,25 @@
         copies.append(copy)
     norm_got[side] = norm_own[...]
 
+    turn = (iota((SUB, SUB), 0) + iota((SUB, SUB), 1) == SUB - 1).astype(F32).astype(BF16)
+
     def tables_of(j):
         start = jnp.exp(-rate_wide(j) * offset)
         taps = jnp.sum(res_wide(j) * start, axis=0, keepdims=True)
         toeplitz = jnp.where(lane_id >= row_id, strided(taps, 0), 0.0)
-        return halves(jnp.concatenate([start, start * offset], axis=0)) + halves(toeplitz)
-
-    def tables_put(j, high, low, toeplitz_high, toeplitz_low):
+        turned = tuple(
+            dot(
+                turn,
+                jnp.concatenate([part[n * SUB : (n + 1) * SUB] for n in range(subs)], axis=1),
+            ).astype(BF16)
+            for part in halves(signal_of(j))
+        )
+        return (
+            halves(jnp.concatenate([start, start * offset], axis=0)) + halves(toeplitz) + turned
+        )
+
+    def tables_put(j, high, low, toeplitz_high, toeplitz_low, turned_high, turned_low):
+        turned_s[j, 0], turned_s[j, 1] = turned_high, turned_low
         table_s[j, 0], table_s[j, 1] = high, low
         toeplitz_s[j, 0], toeplitz_s[j, 1] = toeplitz_high, toeplitz_low
 
@@ -459,7 +499,6 @@
     wide_to_group = (
         iota((wide, groups), 0) // SUB == iota((wide, groups), 1)
     ).astype(F32).astype(BF16)
-    half_row = iota((SUB, LANES), 0)
 
     def weight_of(j):
         at = lanes(j)
@@ -495,20 +534,18 @@
         back = product((toeplitz_s[j, 0], toeplitz_s[j, 1]), right)
         back = jnp.concatenate([back[:, n * LANES : (n + 1) * LANES] for n in range(subs)], axis=0)
 
-        left = tuple(
-            jnp.concatenate([part[n * SUB : (n + 1) * SUB] for n in range(subs)], axis=1)
-            for part in halves(signal_of(j))
-        )
-        pairs = jnp.where(lane_id >= row_id, product(left, right, dot_t), 0.0)
-        lagged = []
-        for h in range(wide // LANES):
-            part = pairs[:, h * LANES : (h + 1) * LANES]
-            bit = 1
-            while bit < SUB:
-                moved = pltpu.roll(part, LANES - bit, 1)
-                part = jnp.where((half_row // bit) % 2 == 1, moved, part)
-                bit *= 2
-            lagged.append(jnp.sum(part, axis=0, keepdims=True))
+        pairs = product((turned_s[j, 0], turned_s[j, 1]), right, dot_t)
+        pairs = jnp.where(lane_id + row_id >= SUB - 1, pairs, 0.0)
+        lagged = [
+            jnp.sum(
+                pltpu.roll(
+                    pairs[:, h * LANES : (h + 1) * LANES], LANES - SUB + 1, 1, stride=1, stride_axis=0
+                ),
+                axis=0,
+                keepdims=True,
+            )
+            for h in range(wide // LANES)
+        ]
         zeroth = start * jnp.concatenate(lagged, axis=1)
         local = jnp.concatenate([zeroth, zeroth * offset], axis=0)
 
@@ -569,9 +606,9 @@
         gv_ref[:, lanes(j)] = grad_v
 
     blocks_then_send(weight_of, weight_put, own_b, in_b, 2)
-    batches(inside_of, inside_put, 0, half, 2)
+    batches(inside_of, inside_put, 0, half, 4)
     join(own_b, in_b, out_b, got_b, 2, True)
-    batches(inside_of, inside_put, half, blocks, 2)
+    batches(inside_of, inside_put, half, blocks, 4)
     stores = [
         pltpu.make_async_copy(mixer_ref, mixer_out, store_sem.at[0]),
         pltpu.make_async_copy(gq_ref, gq_out, store_sem.at[1]),
@@ -628,15 +665,21 @@
 
 
 def finish(*refs):
-    sources, targets, sems = refs[:6], refs[6:12], refs[12]
-    copies = [
-        pltpu.make_async_copy(source, target, sems.at[k])
-        for k, (source, target) in enumerate(zip(sources, targets))
-    ]
-    for copy in copies:
-        copy.start()
-    for copy in copies:
-        copy.wait()
+    sources, targets, held, (load_sem, store_sem) = refs[:6], refs[6:12], refs[12:18], refs[18:]
+    loads, stores = [], []
+    for k, (source, target, middle) in enumerate(zip(sources, targets, held)):
+        rows = min(source.shape[0], PART_ROWS)
+        for q in range(source.shape[0] // rows):
+            at = pl.ds(q * rows, rows)
+            loads.append(pltpu.make_async_copy(source.at[at], middle.at[at], load_sem.at[k, q]))
+            stores.append(pltpu.make_async_copy(middle.at[at], target.at[at], store_sem.at[k, q]))
+    for load in loads:
+        load.start()
+    for load, store in zip(loads, stores):
+        load.wait()
+        store.start()
+    for store in stores:
+        store.wait()
 
 
 def per_device(out_gate, key_proj, value_proj, residue, log_decay, skip, gain, cotangent):
@@ -685,6 +728,7 @@
             pltpu.VMEM((blocks, 2 * modes, wide + LANES), F32),
             pltpu.VMEM((blocks, 2, 2 * modes, wide), BF16),
             pltpu.VMEM((blocks, 2, SUB, wide), BF16),
+            pltpu.VMEM((blocks, 2, SUB, subs * LANES), BF16),
             pltpu.VMEM((blocks, 2 * modes, wide), F32),
             pltpu.VMEM((blocks, 2 * modes, LANES), F32),
             pltpu.VMEM((2, blocks, LANES), F32),
@@ -713,7 +757,8 @@
         out_shape=results,
         in_specs=[hbm] * 6,
         out_specs=[hbm] * 6,
-        scratch_shapes=[pltpu.SemaphoreType.DMA((6,))],
+        scratch_shapes=[pltpu.VMEM(result.shape, result.dtype) for result in results]
+        + [pltpu.SemaphoreType.DMA((6, length // PART_ROWS))] * 2,
         compiler_params=pltpu.CompilerParams(vmem_limit_bytes=60 * 1024 * 1024),
         name="finish",
     )(*computed)

time: 106 us -> 40.6 us (0.38)
  Pallas kernels: 105 us -> 39.8 us
    pallas_call x1, Pallas kernels: 65.2 us -> 2.47 us  [per_device(): pl.pallas_call(finish, out_shape=results, in_specs=[hbm] * 6, out_specs=[...]
    pallas_call x1, Pallas kernels: 39.9 us -> 37.3 us  [per_device(): pl.pallas_call(functools.partial(kernel, ctx_count, tp_count, float(chann...]
where the time goes in v4:
time: 40.6 us; the launch traced here: 40.4 us
  Pallas kernels  39.8 us (98%)
  between operations  0.64 us (2%)
    pallas_call x1, Pallas kernels, per_device(): pl.pallas_call(functools.partial(kernel, ctx_count, tp_count, float(chann...  37.3 us
    pallas_call x1, Pallas kernels, per_device(): pl.pallas_call(finish, out_shape=results, in_specs=[hbm] * 6, out_specs=[...  2.47 us

profile of v4, /device:TPU:0, one launch (start us, length us, event | category | flops | bytes accessed | tf_op | source)
XLA Modules:
  0.0 40.4 jit_solution(13702889200776896811)
XLA Ops:
  0.6 37.3 %mixer.1 = (bf16[128,2048]{1,0:T(8,128)(2,1)}, bf16[128,2048]{1,0:T(8,128)(2,1)}, bf16[128,2048]{1,0:T(8,128)(2,1)}, bf16[128,2048]{1,0:T(8,128)(2,1)}, f32[16,128]{1,0:T(8,128)}, /*index=5*/f32[16,128]{1,0:T(8,128)}) custom-call(bf16[128,2048]{1,0:T(8,128)(2,1)} %gate_in.1, bf16[128,2048]{1,0:T(8,128)(2,1)} %key_in.1, bf16[128,2048]{1,0:T(8,128)(2,1)} %value_in.1, ...), custom_call_target="tpu_custom_call" | custom-call | tf_op jit(solution)/shard_map/mixer/pallas_call | solution.py:700
  37.9 2.5 %finish.1 = (bf16[128,2048]{1,0:T(8,128)(2,1)}, bf16[128,2048]{1,0:T(8,128)(2,1)}, bf16[128,2048]{1,0:T(8,128)(2,1)}, bf16[128,2048]{1,0:T(8,128)(2,1)}, f32[16,128]{1,0:T(8,128)}, /*index=5*/f32[16,128]{1,0:T(8,128)}) custom-call(bf16[128,2048]{1,0:T(8,128)(2,1)} %get-tuple-element.18.refs_0_, bf16[128,2048]{1,0:T(8,128)(2,1)} %get-tuple-element.19.refs_1_, ...), custom_call_target="tpu_custom_call" | custom-call | tf_op jit(solution)/shard_map/finish/pallas_call | solution.py:755

commit v5 on v4

--- a/solution.py
+++ b/solution.py
@@ -35,14 +35,10 @@
     return both[:rows] + both[rows:] + multiply(left[0], right[1])
 
 
-def exact_dot(value, ones):
+def ones_dot(value, ones):
     rows = value.shape[0]
-    high, rest = value.astype(BF16), None
-    rest = value - high.astype(F32)
-    mid = rest.astype(BF16)
-    low = (rest - mid.astype(F32)).astype(BF16)
-    out = dot(jnp.concatenate([high, mid, low], axis=0), ones)
-    return out[:rows] + out[rows : 2 * rows] + out[2 * rows :]
+    out = dot(jnp.concatenate(halves(value), axis=0), ones)
+    return out[:rows] + out[rows:]
 
 
 def iota(shape, dim):
@@ -121,6 +117,8 @@
     norm_got,
     part_s,
     part_got,
+    sum_s,
+    sum_got,
     send_sem,
     recv_sem,
     tp_send,
@@ -140,6 +138,8 @@
     wide = in_block * SUB
     piece_rows = blocks * modes // ctx_count
     per = piece_rows // modes
+    shared = (2 * modes) % ctx_count == 0
+    part_rows = 2 * modes // ctx_count
 
     loads = [
         pltpu.make_async_copy(source, target, load_sem.at[k])
@@ -363,8 +363,8 @@
     rolled = [
         pltpu.roll(tables, (groups - j * in_block) % groups, 1) for j in range(blocks)
     ]
-    wide_s[...] = exact_dot(jnp.concatenate(rolled, axis=0), widen[...]).reshape(wide_s.shape)
-    flat = exact_dot(jnp.concatenate([rates, residues], axis=0), spread_modes)
+    wide_s[...] = ones_dot(jnp.concatenate(rolled, axis=0), widen[...]).reshape(wide_s.shape)
+    flat = ones_dot(jnp.concatenate([rates, residues], axis=0), spread_modes)
     for q in range(2):
         for j in range(blocks):
             first = q * groups + j * in_block
@@ -430,6 +430,28 @@
         acc_s[0] += square
         acc_s[1] += inner
 
+    turn = (iota((SUB, SUB), 0) + iota((SUB, SUB), 1) == SUB - 1).astype(F32).astype(BF16)
+
+    def tables_of(j):
+        start = jnp.exp(-rate_wide(j) * offset)
+        taps = jnp.sum(res_wide(j) * start, axis=0, keepdims=True)
+        toeplitz = jnp.where(lane_id >= row_id, strided(taps, 0), 0.0)
+        turned = tuple(
+            dot(
+                turn,
+                jnp.concatenate([part[n * SUB : (n + 1) * SUB] for n in range(subs)], axis=1),
+            ).astype(BF16)
+            for part in halves(signal_of(j))
+        )
+        return (
+            halves(jnp.concatenate([start, start * offset], axis=0)) + halves(toeplitz) + turned
+        )
+
+    def tables_put(j, high, low, toeplitz_high, toeplitz_low, turned_high, turned_low):
+        turned_s[j, 0], turned_s[j, 1] = turned_high, turned_low
+        table_s[j, 0], table_s[j, 1] = high, low
+        toeplitz_s[j, 0], toeplitz_s[j, 1] = toeplitz_high, toeplitz_low
+
     for load in loads[2:4]:
         load.wait()
     pl.semaphore_wait(barrier, ctx_count - 1 + tp_count - 1)
@@ -439,6 +461,7 @@
     batches(local_of, local_put, 0, half, 4)
     join(own_s, in_s, out_s, got_s, 0, False)
     batches(local_of, local_put, half, blocks, 4)
+    batches(tables_of, tables_put, 0, half, 4)
     for load in loads[5:]:
         load.wait()
     receive_then_blocks(carried_of, carried_put, out_s, got_s, 1)
@@ -460,29 +483,7 @@
         copies.append(copy)
     norm_got[side] = norm_own[...]
 
-    turn = (iota((SUB, SUB), 0) + iota((SUB, SUB), 1) == SUB - 1).astype(F32).astype(BF16)
-
-    def tables_of(j):
-        start = jnp.exp(-rate_wide(j) * offset)
-        taps = jnp.sum(res_wide(j) * start, axis=0, keepdims=True)
-        toeplitz = jnp.where(lane_id >= row_id, strided(taps, 0), 0.0)
-        turned = tuple(
-            dot(
-                turn,
-                jnp.concatenate([part[n * SUB : (n + 1) * SUB] for n in range(subs)], axis=1),
-            ).astype(BF16)
-            for part in halves(signal_of(j))
-        )
-        return (
-            halves(jnp.concatenate([start, start * offset], axis=0)) + halves(toeplitz) + turned
-        )
-
-    def tables_put(j, high, low, toeplitz_high, toeplitz_low, turned_high, turned_low):
-        turned_s[j, 0], turned_s[j, 1] = turned_high, turned_low
-        table_s[j, 0], table_s[j, 1] = high, low
-        toeplitz_s[j, 0], toeplitz_s[j, 1] = toeplitz_high, toeplitz_low
-
-    batches(tables_of, tables_put, 0, blocks, 4)
+    batches(tables_of, tables_put, half, blocks, 4)
     for copy in copies:
         copy.wait()
     sums = norm_got[0]
@@ -579,7 +580,7 @@
         cross_s[j, modes:] = moment
 
     def group_sums(ref, ones):
-        rows = exact_dot(ref[...].reshape(blocks * 2 * modes, ref.shape[2]), ones)
+        rows = ones_dot(ref[...].reshape(blocks * 2 * modes, ref.shape[2]), ones)
         total = rows[: 2 * modes]
         for j in range(1, blocks):
             total += pltpu.roll(rows[2 * modes * j : 2 * modes * (j + 1)], j * in_block, 1)
@@ -617,9 +618,16 @@
         store.start()
     inside_total = group_sums(local_s, wide_to_group)
     receive_then_blocks(ending_of, ending_put, out_b, got_b, 3)
-    part_s[...] = inside_total + group_sums(cross_s, to_group)
-    all_others(lambda d: transfer(part_s, part_got, 4, d, False).start())
-    part_got[here] = part_s[...]
+    total = inside_total + group_sums(cross_s, to_group)
+    if shared:
+        for k in range(ctx_count):
+            part_s[k] = total[k * part_rows : (k + 1) * part_rows]
+        all_others(lambda d: transfer(part_s, part_got, 4, d).start())
+        part_got[here] = part_s[here]
+    else:
+        part_s[...] = total
+        all_others(lambda d: transfer(part_s, part_got, 4, d, False).start())
+        part_got[here] = part_s[...]
 
     size = 4
 
@@ -636,11 +644,19 @@
             store.start()
         return 0
 
-    lax.fori_loop(0, blocks // size, grads, 0)
-    all_others(lambda d: transfer(part_s, part_got, 4, d, False).wait())
+    lax.fori_loop(0, blocks // size // 2, grads, 0)
+    all_others(lambda d: transfer(part_s, part_got, 4, d, shared).wait_recv())
     sums = part_got[0]
     for k in range(1, ctx_count):
         sums = sums + part_got[k]
+    if shared:
+        sum_s[...] = sums
+        all_others(lambda d: transfer(sum_s, sum_got, 5, d, False).start())
+        sum_got[here] = sums
+    lax.fori_loop(blocks // size // 2, blocks // size, grads, 0)
+    if shared:
+        all_others(lambda d: transfer(sum_s, sum_got, 5, d, False).wait())
+        sums = jnp.concatenate([sum_got[k] for k in range(ctx_count)], axis=0)
     scale = 1.0 / (length * ctx_count)
     filt_ref[:modes] = sums[:modes] * scale
     filt_ref[modes:] = -res_ref[...] * jnp.exp(log_ref[...]) * sums[modes:] * scale
@@ -652,6 +668,7 @@
         store.start()
 
     def drain(d):
+        transfer(part_s, part_got, 4, d, shared).wait_send()
         for phase, (source, target) in enumerate(
             ((own_s, in_s), (out_s, got_s), (own_b, in_b), (out_b, got_b))
         ):
@@ -692,6 +709,9 @@
     subs = length // SUB
     wide = in_block * SUB
     piece_rows = blocks * modes // ctx_count
+    part_shape = (2 * modes, groups)
+    if (2 * modes) % ctx_count == 0:
+        part_shape = (ctx_count, 2 * modes // ctx_count, groups)
     pieces = pltpu.VMEM((ctx_count, piece_rows, LANES), F32)
     wide_out = jax.ShapeDtypeStruct((length, channels), BF16)
     table_out = jax.ShapeDtypeStruct((modes, groups), F32)
@@ -737,10 +757,12 @@
             pieces, pieces, pieces, pieces,
             pltpu.VMEM((8, length), F32),
             pltpu.VMEM((tp_count, 8, length), F32),
-            pltpu.VMEM((2 * modes, groups), F32),
-            pltpu.VMEM((ctx_count, 2 * modes, groups), F32),
-            pltpu.SemaphoreType.DMA((5, ctx_count)),
-            pltpu.SemaphoreType.DMA((5, ctx_count)),
+            pltpu.VMEM(part_shape, F32),
+            pltpu.VMEM((ctx_count,) + part_shape[-2:], F32),
+            pltpu.VMEM(part_shape[-2:], F32),
+            pltpu.VMEM((ctx_count,) + part_shape[-2:], F32),
+            pltpu.SemaphoreType.DMA((6, ctx_count)),
+            pltpu.SemaphoreType.DMA((6, ctx_count)),
             pltpu.SemaphoreType.DMA((tp_count,)),
             pltpu.SemaphoreType.DMA((tp_count,)),
             pltpu.SemaphoreType.DMA((8,)),

time: 40.6 us -> 44.8 us (1.10)
  Pallas kernels: 39.8 us -> 44 us
    pallas_call x1, Pallas kernels: 37.3 us -> 41.5 us  [per_device(): pl.pallas_call(functools.partial(kernel, ctx_count, tp_count, float(chann...]
where the time goes in v5:
time: 44.8 us; the launch traced here: 44.6 us
  Pallas kernels  44 us (98%)
  between operations  0.64 us (1%)
    pallas_call x1, Pallas kernels, per_device(): pl.pallas_call(functools.partial(kernel, ctx_count, tp_count, float(chann...  41.5 us
    pallas_call x1, Pallas kernels, per_device(): pl.pallas_call(finish, out_shape=results, in_specs=[hbm] * 6, out_specs=[...  2.47 us

profile of v5, /device:TPU:0, one launch (start us, length us, event | category | flops | bytes accessed | tf_op | source)
XLA Modules:
  0.0 44.6 jit_solution(4740158571147840190)
XLA Ops:
  0.6 41.5 %mixer.1 = (bf16[128,2048]{1,0:T(8,128)(2,1)}, bf16[128,2048]{1,0:T(8,128)(2,1)}, bf16[128,2048]{1,0:T(8,128)(2,1)}, bf16[128,2048]{1,0:T(8,128)(2,1)}, f32[16,128]{1,0:T(8,128)}, /*index=5*/f32[16,128]{1,0:T(8,128)}) custom-call(bf16[128,2048]{1,0:T(8,128)(2,1)} %gate_in.1, bf16[128,2048]{1,0:T(8,128)(2,1)} %key_in.1, bf16[128,2048]{1,0:T(8,128)(2,1)} %value_in.1, ...), custom_call_target="tpu_custom_call" | custom-call | tf_op jit(solution)/shard_map/mixer/pallas_call | solution.py:720
  42.1 2.5 %finish.1 = (bf16[128,2048]{1,0:T(8,128)(2,1)}, bf16[128,2048]{1,0:T(8,128)(2,1)}, bf16[128,2048]{1,0:T(8,128)(2,1)}, bf16[128,2048]{1,0:T(8,128)(2,1)}, f32[16,128]{1,0:T(8,128)}, /*index=5*/f32[16,128]{1,0:T(8,128)}) custom-call(bf16[128,2048]{1,0:T(8,128)(2,1)} %get-tuple-element.18.refs_0_, bf16[128,2048]{1,0:T(8,128)(2,1)} %get-tuple-element.19.refs_1_, ...), custom_call_target="tpu_custom_call" | custom-call | tf_op jit(solution)/shard_map/finish/pallas_call | solution.py:777

commit v6 on v4

--- a/solution.py
+++ b/solution.py
@@ -35,14 +35,10 @@
     return both[:rows] + both[rows:] + multiply(left[0], right[1])
 
 
-def exact_dot(value, ones):
+def ones_dot(value, ones):
     rows = value.shape[0]
-    high, rest = value.astype(BF16), None
-    rest = value - high.astype(F32)
-    mid = rest.astype(BF16)
-    low = (rest - mid.astype(F32)).astype(BF16)
-    out = dot(jnp.concatenate([high, mid, low], axis=0), ones)
-    return out[:rows] + out[rows : 2 * rows] + out[2 * rows :]
+    out = dot(jnp.concatenate(halves(value), axis=0), ones)
+    return out[:rows] + out[rows:]
 
 
 def iota(shape, dim):
@@ -363,8 +359,8 @@
     rolled = [
         pltpu.roll(tables, (groups - j * in_block) % groups, 1) for j in range(blocks)
     ]
-    wide_s[...] = exact_dot(jnp.concatenate(rolled, axis=0), widen[...]).reshape(wide_s.shape)
-    flat = exact_dot(jnp.concatenate([rates, residues], axis=0), spread_modes)
+    wide_s[...] = ones_dot(jnp.concatenate(rolled, axis=0), widen[...]).reshape(wide_s.shape)
+    flat = ones_dot(jnp.concatenate([rates, residues], axis=0), spread_modes)
     for q in range(2):
         for j in range(blocks):
             first = q * groups + j * in_block
@@ -579,7 +575,7 @@
         cross_s[j, modes:] = moment
 
     def group_sums(ref, ones):
-        rows = exact_dot(ref[...].reshape(blocks * 2 * modes, ref.shape[2]), ones)
+        rows = ones_dot(ref[...].reshape(blocks * 2 * modes, ref.shape[2]), ones)
         total = rows[: 2 * modes]
         for j in range(1, blocks):
             total += pltpu.roll(rows[2 * modes * j : 2 * modes * (j + 1)], j * in_block, 1)

time: 40.6 us -> 40.6 us (level)
  no operation moved by 1% of the time
where the time goes in v6:
time: 40.6 us; the launch traced here: 40.4 us
  Pallas kernels  39.7 us (98%)
  between operations  0.64 us (2%)
    pallas_call x1, Pallas kernels, per_device(): pl.pallas_call(functools.partial(kernel, ctx_count, tp_count, float(chann...  37.2 us
    pallas_call x1, Pallas kernels, per_device(): pl.pallas_call(finish, out_shape=results, in_specs=[hbm] * 6, out_specs=[...  2.47 us

profile of v6, /device:TPU:0, one launch (start us, length us, event | category | flops | bytes accessed | tf_op | source)
XLA Modules:
  0.0 40.4 jit_solution(15612609668784175625)
XLA Ops:
  0.6 37.2 %mixer.1 = (bf16[128,2048]{1,0:T(8,128)(2,1)}, bf16[128,2048]{1,0:T(8,128)(2,1)}, bf16[128,2048]{1,0:T(8,128)(2,1)}, bf16[128,2048]{1,0:T(8,128)(2,1)}, f32[16,128]{1,0:T(8,128)}, /*index=5*/f32[16,128]{1,0:T(8,128)}) custom-call(bf16[128,2048]{1,0:T(8,128)(2,1)} %gate_in.1, bf16[128,2048]{1,0:T(8,128)(2,1)} %key_in.1, bf16[128,2048]{1,0:T(8,128)(2,1)} %value_in.1, ...), custom_call_target="tpu_custom_call" | custom-call | tf_op jit(solution)/shard_map/mixer/pallas_call | solution.py:696
  37.9 2.5 %finish.1 = (bf16[128,2048]{1,0:T(8,128)(2,1)}, bf16[128,2048]{1,0:T(8,128)(2,1)}, bf16[128,2048]{1,0:T(8,128)(2,1)}, bf16[128,2048]{1,0:T(8,128)(2,1)}, f32[16,128]{1,0:T(8,128)}, /*index=5*/f32[16,128]{1,0:T(8,128)}) custom-call(bf16[128,2048]{1,0:T(8,128)(2,1)} %get-tuple-element.18.refs_0_, bf16[128,2048]{1,0:T(8,128)(2,1)} %get-tuple-element.19.refs_1_, ...), custom_call_target="tpu_custom_call" | custom-call | tf_op jit(solution)/shard_map/finish/pallas_call | solution.py:751
